TPU v7x, 32 devices: a whole 2x2x4 slice. The times are simulated.
32 devices in a mesh: sta: 8 (over z, y), tpl: 4 (over x, core).
Axes of the slice: x: 2, y: 2, z: 4, core: 2. Of those that a mesh axis runs over, the one named last changes fastest.
Arguments:
- window: bfloat16 [384, 1024], P('sta', 'tpl'), may hold values from -6 to 6
- prior: bfloat16 [384, 599], P('sta'), may hold values from -6 to 6
- waves: bfloat16 [32, 128, 600], P('tpl', 'sta'), may hold values from -6 to 6
- chan_list: int32 [32, 128], P('tpl', 'sta'), may hold values from 0 to 383, as said below
- chan_count: int32 [32], P('tpl'), may hold values from 21 to 120
- station_row: int32 [128], replicated, may hold values from 0 to 127, as said below
Outputs:
- stacked: float32 [32, 1024], P(('tpl', 'sta'))
Inputs may be any that keep to these rules, and one draw needn't show every extreme that they name: station_row is a permutation of 0 to 127; station s's three channels are data rows 3 station_row[s] to 3 station_row[s] + 2, and its station block is station_row[s] // 16. `chan_list`: channel c is component c % 3 of station c // 3. For every group of 8 templates (g * 8 to (g + 1) * 8 - 1) and every aligned run of 16 slots, each station block is named by exactly 16 of those slots, listed or not.
All inputs are finite; a program needn't handle non-finite values.
Results may differ from a plain program's by a relative error of at most 0.0029.
Values may be sent and summed in bfloat16 or wider, within the bound.
No kernel may reach another device: no remote copies, remote signals or barrier semaphores. Data moves between devices by JAX's collectives and lax.ppermute only.
A program may use at most 64 MiB of HBM per device.

v0:
```python
import jax
import jax.numpy as jnp
from jax import lax
from jax.sharding import PartitionSpec as P

epsilon = 1e-06


def correlate(data_rows, wave_rows):
    result = lax.conv_general_dilated(
        data_rows[None],
        wave_rows[:, None, :],
        (1,),
        "VALID",
        dimension_numbers=("NCH", "OIH", "NCH"),
        feature_group_count=data_rows.shape[0],
        preferred_element_type=jnp.float32,
    )
    return result[0]


def inverse_energy(rows, lag_count, length):
    squares = rows.astype(jnp.float32) ** 2
    prefix = jnp.concatenate(
        [jnp.zeros((rows.shape[0], 1), jnp.float32), jnp.cumsum(squares, axis=1)], axis=1
    )
    energy = prefix[:, length : length + lag_count] - prefix[:, :lag_count]
    return 1.0 / jnp.sqrt(energy + epsilon)


def unit_waves(waves, listed):
    raw_wave = waves.astype(jnp.float32)
    wave_norms = jnp.sqrt(jnp.sum(raw_wave * raw_wave, axis=-1, keepdims=True) + epsilon)
    return (raw_wave / wave_norms * listed[..., None]).astype(jnp.bfloat16)


def per_device(window, prior, waves, chan_list, chan_count, station_row):
    sta_size = lax.axis_size("sta")
    sta_pos = lax.axis_index("sta")
    whole_time = lax.all_gather(window, "tpl", axis=1, tiled=True)
    extended = jnp.concatenate([prior, whole_time], axis=1)
    block_rows = extended.shape[0]
    lag_count = whole_time.shape[1]
    length = waves.shape[2]
    group_size, slot_count = chan_list.shape
    positions = group_size * slot_count
    capacity = positions // sta_size
    slot_index = sta_pos * slot_count + jnp.arange(slot_count, dtype=jnp.int32)
    listed = (slot_index[None, :] < chan_count[:, None]).astype(jnp.float32)
    normed = unit_waves(waves, listed).reshape(positions, length)
    flat_list = chan_list.reshape(positions)
    data_rows = 3 * jnp.take(station_row, flat_list // 3) + flat_list % 3
    owners = data_rows // block_rows
    local_rows = data_rows % block_rows
    owner_hits = (owners[:, None] == jnp.arange(sta_size, dtype=jnp.int32)[None, :]).astype(
        jnp.int32
    )
    rank_in = jnp.sum(jnp.cumsum(owner_hits, axis=0) * owner_hits, axis=1) - 1
    slot_at = owners * capacity + rank_in
    order_of = (
        jnp.zeros((positions,), jnp.int32).at[slot_at].set(jnp.arange(positions, dtype=jnp.int32))
    )
    template_of = jnp.arange(positions, dtype=jnp.int32) // slot_count
    sent_waves = normed[order_of]
    requests = (template_of * block_rows + local_rows)[order_of].reshape(sta_size, capacity)
    asked_rows = lax.all_to_all(requests, "sta", split_axis=0, concat_axis=0, tiled=True).reshape(
        positions
    )
    arrived = lax.all_to_all(
        sent_waves.reshape(sta_size, capacity, length),
        "sta",
        split_axis=0,
        concat_axis=0,
        tiled=True,
    ).reshape(positions, length)
    wanted = asked_rows % block_rows
    block_scales = inverse_energy(extended, lag_count, length)
    traces = correlate(extended[wanted], arrived) * block_scales[wanted]
    buffer_templates = asked_rows // block_rows
    selector = (
        buffer_templates[None, :] == jnp.arange(group_size, dtype=jnp.int32)[:, None]
    ).astype(jnp.float32)
    return lax.psum_scatter(
        jnp.dot(
            selector, traces, precision=lax.Precision.HIGHEST, preferred_element_type=jnp.float32
        ),
        "sta",
        scatter_dimension=0,
        tiled=True,
    )


def solution(mesh):
    in_specs = (
        P("sta", "tpl"),
        P("sta", None),
        P("tpl", "sta", None),
        P("tpl", "sta"),
        P("tpl"),
        P(),
    )
    out_specs = P(("tpl", "sta"), None)
    return jax.shard_map(
        per_device, mesh=mesh, in_specs=in_specs, out_specs=out_specs, check_vma=False
    )
```

profile of v0, /device:TPU:0, one launch (start us, length us, event | category | flops | bytes accessed | tf_op | source)
XLA Modules:
  0.0 334.2 jit_solution(6184463301516415176)
XLA Ops:
  0.0 0.8 broadcast_divide_fusion
  0.8 0.1 div.75
  0.9 0.1 div.74
  0.9 0.1 rem.92
  1.0 0.1 rem.91
  1.1 0.1 ne.172
  1.2 0.1 ne.170
  1.3 1.2 gather_fusion
  2.6 0.1 fusion.8
  2.7 0.2 reduce_window_sum.26
  2.8 0.2 select_reduce_fusion
  3.1 1.0 scatter_custom_fusion
  4.1 1.2 gather_fusion.1
  5.3 0.7 all_to_all.9
  6.0 7.3 %all-to-all-start = ((s32[8,1,16]{2,1,0:T(1,128)}), s32[8,1,16]{2,1,0:T(1,128)S(1)}, u32[]{:S(2)}, u32[]{:S(2)}) async-start(s32[8,1,16]{2,1,0:T(1,128)} %bitcast.4), calls=%async_computation | async-start | bytes 8192 | tf_op jit(solution)/shard_map/all_to_all | solution.py:66
  13.3 5.3 %all_gather.3 = bf16[48,1024]{1,0:T(8,128)(2,1)S(1)} all-gather(bf16[48,256]{1,0:T(8,128)(2,1)S(1)} %copy-done.3), channel_id=1, replica_groups=mesh['sta'=8,'tpl'=4] {'tpl'}, dimensions={1}, use_global_device_ids=true | all-gather | bytes 122880 | tf_op jit(solution)/shard_map/all_gather | solution.py:40
  18.6 0.1 fusion.2
  18.8 0.7 copy-done.2
  19.5 0.1 convert_multiply_fusion.1
  19.6 0.1 reshape.304
  19.7 13.6 %reduce-window.6 = f32[48,13,128]{2,1,0:T(8,128)S(1)} reduce-window(f32[48,13,128]{2,1,0:T(8,128)S(1)} %reshape.304, f32[]{:T(128)} %constant.93.clone.1), window={size=1x1x128 pad=0_0x0_0x127_0}, to_apply=%region_4.5 | reduce-window | flops 10143744 | bytes 638980 | tf_op jit(solution)/shard_map/reduce-window
  33.3 0.2 slice.31
  33.5 0.2 copy.24
  33.7 0.1 copy.25
  33.8 0.2 broadcast_add_fusion
  34.0 0.1 copy.29
  34.1 0.2 fusion.7
  34.3 0.5 copy-done.5
  34.8 0.1 compare_convert_fusion
  34.8 0.1 fusion.4
  35.0 0.1 pad_maximum_fusion
  35.1 1.5 gather_fusion.3
  36.6 0.7 copy-done.6
  37.3 0.6 dynamic-slice
  37.9 6.0 %all-to-all-start.1 = ((bf16[8,16,600]{2,1,0:T(8,128)(2,1)}), bf16[8,16,600]{2,1,0:T(8,128)(2,1)S(1)}, u32[]{:S(2)}, u32[]{:S(2)}) async-start(bf16[8,16,600]{2,1,0:T(8,128)(2,1)} %bitcast.8), calls=%async_computation.1 | async-start | bytes 327680 | tf_op jit(solution)/shard_map/all_to_all | solution.py:69
  43.9 0.1 rem.99
  44.1 1.0 gather_fusion.2
  45.0 1.3 copy.22
  46.3 0.1 div.79
  46.4 0.1 and.111
  46.5 0.8 gather_fusion.4
  47.3 0.2 copy.26
  47.5 4.3 %all-to-all-done.1 = bf16[8,16,600]{2,1,0:T(8,128)(2,1)S(1)} async-done(((bf16[8,16,600]{2,1,0:T(8,128)(2,1)}), bf16[8,16,600]{2,1,0:T(8,128)(2,1)S(1)}, u32[]{:S(2)}, u32[]{:S(2)}) %all-to-all-start.1) | async-done | bytes 153632 | tf_op jit(solution)/shard_map/all_to_all | solution.py:69
  51.8 0.2 copy.23
  52.1 246.1 %fusion.19 = f32[1,128,1024]{1,0,2:T(1,128)S(1)} fusion(bf16[1,128,1623]{1,0,2:T(2,128)(2,1)S(1)} %copy.22, bf16[128,1,600]{0,1,2:T(2,128)(2,1)S(1)} %copy.23), kind=kOutput, calls=%fused_computation.68 | convolution fusion | flops 157286400 | bytes 1093376 | tf_op jit(solution)/shard_map/conv_general_dilated | solution.py:10
  298.1 0.4 fusion
  298.5 34.5 %all-reduce.2 = f32[8,1024]{1,0:T(8,128)S(1)} all-reduce(f32[8,1024]{1,0:T(8,128)S(1)} %fusion), channel_id=2, replica_groups=mesh['sta'=8,'tpl'=4] {'sta'}, use_global_device_ids=true, to_apply=%region_6.7.clone | all-reduce | flops 8192 | bytes 65536
  333.0 1.2 constant_dynamic-slice_fusion
  (30 shorter events, 0.3 us)
Async XLA Ops:
  0.0 1.3 copy-start
  0.0 0.8 copy-start.4
  4.1 9.2 %copy-start.3 = (bf16[48,256]{1,0:T(8,128)(2,1)S(1)}, bf16[48,256]{1,0:T(8,128)(2,1)}, u32[]{:S(2)}) copy-start(bf16[48,256]{1,0:T(8,128)(2,1)} %param.6) | copy-start | bytes 73732
  4.1 14.5 %copy-start.1 = (bf16[8,16,600]{2,1,0:T(8,128)(2,1)S(1)}, bf16[8,16,600]{2,1,0:T(8,128)(2,1)}, u32[]{:S(2)}) copy-start(bf16[8,16,600]{2,1,0:T(8,128)(2,1)} %param.8) | copy-start | bytes 460804
  6.0 31.9 %all-to-all-start = ((s32[8,1,16]{2,1,0:T(1,128)}), s32[8,1,16]{2,1,0:T(1,128)S(1)}, u32[]{:S(2)}, u32[]{:S(2)}) async-start(s32[8,1,16]{2,1,0:T(1,128)} %bitcast.4), calls=%async_computation | async-start | bytes 8192 | tf_op jit(solution)/shard_map/all_to_all | solution.py:66
  18.6 0.8 copy-start.2
  34.1 0.7 copy-start.5
  36.6 0.7 copy-start.6
  37.9 14.0 %all-to-all-start.1 = ((bf16[8,16,600]{2,1,0:T(8,128)(2,1)}), bf16[8,16,600]{2,1,0:T(8,128)(2,1)S(1)}, u32[]{:S(2)}, u32[]{:S(2)}) async-start(bf16[8,16,600]{2,1,0:T(8,128)(2,1)} %bitcast.8), calls=%async_computation.1 | async-start | bytes 327680 | tf_op jit(solution)/shard_map/all_to_all | solution.py:69
where the time goes:
time: 335 us; the launch traced here: 334 us
  matrix products  246 us (73%)
  blocking collectives  39.9 us (12%)
  other arithmetic  15.9 us (5%)
  local copies, waits for them, and re-layouts  14.2 us (4%)
  starting transfers between devices  13.3 us (4%)
  waiting for transfers between devices  4.34 us (1%)
    conv_general_dilated x1, matrix products, correlate(): lax.conv_general_dilated(data_rows[None], wave_rows[:, None, :], (1,), 'V...  246 us
    unnamed x1, blocking collectives  34.5 us
    another operation x3, other arithmetic  13.8 us
    all_to_all x1, starting transfers between devices, per_device(): lax.all_to_all(requests, 'sta', split_axis=0, concat_axis=0, tiled=True)  7.28 us
  transfers between devices with their start and end apart: 2, of which 1 were waited for; matrix products, arithmetic and copies ran while one was open for 6% of the time, Pallas kernels for 0%

commit v1 on v0

v1 whole, which is shorter than its diff:
```python
import functools

import jax
import jax.numpy as jnp
from jax import lax
from jax.experimental import pallas as pl
from jax.experimental.pallas import tpu as pltpu
from jax.sharding import PartitionSpec as P

epsilon = 1e-06
LANE = 128
STEP = 32
GROUP = 8
TURNS = LANE // STEP
F32, BF16, I32 = jnp.float32, jnp.bfloat16, jnp.int32


def up(value, unit):
    return -(-value // unit) * unit


def column_sum(values):
    return jnp.sum(values, axis=1, keepdims=True)


def route_kernel(
    sta_size, block_rows, sta_pos, waves, chan_list, chan_count, station_row, sent, padded
):
    positions, length = waves.shape
    group_size, slot_count = chan_list.shape
    width = sent.shape[1]
    capacity = positions // sta_size
    spot = lax.broadcasted_iota(I32, (positions, 1), 0)
    template = spot // slot_count
    slot = spot % slot_count
    slot_lane = lax.broadcasted_iota(I32, (positions, slot_count), 1)
    named = jnp.zeros((positions, slot_count), I32)
    count = jnp.zeros((positions, 1), I32)
    for t in range(group_size):
        here = template == t
        named = jnp.where(here, chan_list[t : t + 1, :], named)
        count = jnp.where(here, chan_count[t], count)
    channel = column_sum(jnp.where(slot_lane == slot, named.astype(F32), 0.0)).astype(I32)
    station = (channel * 21846) >> 16
    part = channel - 3 * station
    station_lane = lax.broadcasted_iota(I32, (positions, station_row.shape[1]), 1)
    found = column_sum(jnp.where(station_lane == station, station_row[...].astype(F32), 0.0))
    data_row = 3 * found.astype(I32) + part
    owner = jnp.zeros((positions, 1), I32)
    for o in range(1, sta_size):
        owner = owner + (data_row >= o * block_rows).astype(I32)
    local_row = data_row - owner * block_rows
    lane = lax.broadcasted_iota(I32, (positions, LANE), 1)
    row = lax.broadcasted_iota(I32, (positions, LANE), 0)
    hits = (lane == owner).astype(F32)
    before = (lane < row).astype(BF16)
    ahead = jnp.dot(before, hits.astype(BF16), preferred_element_type=F32)
    place = owner * capacity + column_sum(ahead * hits).astype(I32)
    goes = (lane == place).astype(F32).astype(BF16)

    padded[:, width - LANE :] = jnp.zeros((positions, LANE), F32)
    padded[:, :length] = waves[...].astype(F32)
    raw = padded[...]
    listed = (sta_pos[0] * slot_count + slot < count).astype(F32)
    gain = listed / jnp.sqrt(column_sum(raw * raw) + epsilon)
    wide = lax.broadcasted_iota(I32, (positions, width), 1)
    tagged = jnp.where(
        wide == length,
        local_row.astype(F32),
        jnp.where(wide == length + 1, (template ^ owner).astype(F32), raw * gain),
    ).astype(BF16)
    sent[...] = lax.dot_general(
        goes, tagged, (((0,), (0,)), ((), ())), preferred_element_type=F32
    ).astype(BF16)


def prepare_kernel(length, prior, window, shifted, scales, extended):
    rows, before = prior.shape
    lags = window.shape[1]
    total = extended.shape[1]
    start = before // LANE * LANE
    extended[:, :start] = jnp.zeros((rows, start), F32)
    extended[:, start:] = jnp.zeros((rows, total - start), F32)
    extended[:, start : start + lags] = window[...].astype(F32)
    moved = pltpu.roll(extended[:, start:], before - start, axis=1)
    extended[:, start:] = jnp.zeros((rows, total - start), F32)
    extended[:, :before] = prior[...].astype(F32)
    extended[:, start:] = extended[:, start:] + moved
    whole = extended[...]
    used = shifted.shape[2]
    for q in range(2):
        for h in range(2):
            shift = (2 * q + h) * STEP
            turned = whole if shift == 0 else pltpu.roll(whole, total - shift, axis=1)
            shifted[q, h * rows : (h + 1) * rows, :] = turned[:, :used].astype(BF16)
    square = whole * whole
    high = square.astype(BF16)
    low = (square - high.astype(F32)).astype(BF16)
    span = up(length + LANE - 1, LANE)
    sample = lax.broadcasted_iota(I32, (span, LANE), 0)
    lag = lax.broadcasted_iota(I32, (span, LANE), 1)
    band = ((sample >= lag) & (sample < lag + length)).astype(F32).astype(BF16)
    for a in range(lags // LANE):
        at = slice(a * LANE, a * LANE + span)
        energy = jnp.dot(high[:, at], band, preferred_element_type=F32) + jnp.dot(
            low[:, at], band, preferred_element_type=F32
        )
        scale = 1.0 / jnp.sqrt(energy + epsilon)
        for c in range(TURNS):
            turned = scale if c == 0 else pltpu.roll(scale, c * STEP, axis=1)
            turned_high = turned.astype(BF16)
            at = slice(c * rows, (c + 1) * rows)
            scales[at, a * LANE : (a + 1) * LANE] = turned_high
            scales[at, lags + a * LANE : lags + (a + 1) * LANE] = (
                turned - turned_high.astype(F32)
            ).astype(BF16)


def correlate_kernel(length, arrived, shifted, scales, kept, given, frames, waves, traces, toeplitz):
    positions, width = arrived.shape
    rows = scales.shape[0] // TURNS
    lags = scales.shape[1] // 2
    used = shifted.shape[2]
    blocks = lags // LANE
    waves[...] = arrived[...].astype(F32)
    wanted = waves[:, length : length + 1].astype(I32)
    template = waves[:, length + 1 : length + 2].astype(I32)
    turn = lax.broadcasted_iota(I32, (positions, 1), 0) % TURNS
    scale_lane = lax.broadcasted_iota(I32, (positions, TURNS * rows), 1)
    picks = (scale_lane == turn * rows + wanted).astype(F32).astype(BF16)
    group_size = 2 * kept.shape[0]
    lane = lax.broadcasted_iota(I32, (positions, TURNS * group_size), 1)
    chosen = (lane == turn * group_size + template).astype(F32).astype(BF16)

    pairs = wanted.reshape(positions // GROUP, GROUP, 1)
    twice = jnp.concatenate([pairs, pairs + rows], axis=1).reshape(2 * positions, 1)
    picks_twice = (
        (lax.broadcasted_iota(I32, (2 * positions, 2 * rows), 1) == twice).astype(F32).astype(BF16)
    )
    for q in range(2):
        frames[q] = jnp.dot(picks_twice, shifted[q], preferred_element_type=F32).astype(BF16)
    traces[...] = jnp.dot(picks, scales[:, :lags], preferred_element_type=F32) + jnp.dot(
        picks, scales[:, lags:], preferred_element_type=F32
    )
    waves[:, width - LANE :] = jnp.where(
        lax.broadcasted_iota(I32, (positions, LANE), 1) < length - (width - LANE),
        waves[:, width - LANE :],
        0.0,
    )
    low_half = lax.broadcasted_iota(I32, (blocks * GROUP, LANE), 0) % GROUP < GROUP // 2
    lane_block = lax.broadcasted_iota(I32, (blocks * GROUP, LANE), 1) // STEP
    lane_block = (
        lane_block + TURNS - lax.broadcasted_iota(I32, (blocks * GROUP, LANE), 0) % TURNS
    ) % TURNS

    def one_group(g, _):
        first = pl.multiple_of(g * GROUP, GROUP)
        for j in range(GROUP):
            wave = jnp.broadcast_to(waves[pl.ds(first + j, 1), :], (STEP, width))
            toeplitz[j * STEP : (j + 1) * STEP, :] = pltpu.roll(
                wave, 0, axis=1, stride=1, stride_axis=0
            ).astype(BF16)
        at = pl.ds(pl.multiple_of(g * 2 * GROUP, 2 * GROUP), 2 * GROUP)
        data = [
            frames[q, at, a * LANE : a * LANE + width] for q in range(2) for a in range(blocks)
        ]
        product = lax.dot_general(
            jnp.concatenate(data, axis=0),
            toeplitz[...],
            (((1,), (1,)), ((), ())),
            preferred_element_type=F32,
        )
        product = product.reshape(2, blocks, 2, GROUP, 2 * LANE)
        own = jnp.zeros((blocks * GROUP, LANE), F32)
        for q in range(2):
            for h in range(2):
                part = product[q, :, h].reshape(blocks * GROUP, 2 * LANE)
                part = jnp.where(low_half, part[:, :LANE], part[:, LANE:])
                step = 2 * q + h
                if step > 0:
                    part = pltpu.roll(part, step * STEP, axis=1)
                own = jnp.where(lane_block == step, part, own)
        own = own.reshape(blocks, GROUP, LANE)
        for a in range(blocks):
            at_lag = slice(a * LANE, (a + 1) * LANE)
            traces[pl.ds(first, GROUP), at_lag] = traces[pl.ds(first, GROUP), at_lag] * own[a]
        return 0

    lax.fori_loop(0, positions // GROUP, one_group, 0)
    scaled = traces[...]
    high = scaled.astype(BF16)
    low = (scaled - high.astype(F32)).astype(BF16)
    by_template = (((0,), (0,)), ((), ()))
    stacked = lax.dot_general(
        chosen, high, by_template, preferred_element_type=F32
    ) + lax.dot_general(chosen, low, by_template, preferred_element_type=F32)
    for a in range(blocks):
        at_lag = slice(a * LANE, (a + 1) * LANE)
        total = stacked[:group_size, at_lag]
        for c in range(1, TURNS):
            part = stacked[c * group_size : (c + 1) * group_size, at_lag]
            total = total + pltpu.roll(part, LANE - c * STEP, axis=1)
        kept[:, at_lag] = total[: group_size // 2]
        given[:, at_lag] = total[group_size // 2 :]


def per_device(window, prior, waves, chan_list, chan_count, station_row):
    sta_size = lax.axis_size("sta")
    sta_pos = lax.axis_index("sta").astype(I32).reshape(1)
    group_size, slot_count, length = waves.shape
    positions = group_size * slot_count
    block_rows = prior.shape[0]
    width = up(length + STEP, LANE)
    lags = window.shape[1] * lax.axis_size("tpl")
    vmem = pl.BlockSpec(memory_space=pltpu.VMEM)
    smem = pl.BlockSpec(memory_space=pltpu.SMEM)

    sent = pl.pallas_call(
        functools.partial(route_kernel, sta_size, block_rows),
        out_shape=jax.ShapeDtypeStruct((positions, width), BF16),
        in_specs=[smem, vmem, vmem, smem, vmem],
        out_specs=vmem,
        scratch_shapes=[pltpu.VMEM((positions, width), F32)],
        name="route",
    )(
        sta_pos,
        waves.reshape(positions, length),
        chan_list,
        chan_count,
        station_row.reshape(1, station_row.shape[0]),
    )
    arrived = lax.all_to_all(
        sent.reshape(sta_size, positions // sta_size, width),
        "sta",
        split_axis=0,
        concat_axis=0,
        tiled=True,
    ).reshape(positions, width)

    whole_time = lax.all_gather(window, "tpl", axis=1, tiled=True)
    total = up(prior.shape[1] + lags, LANE)
    used = lags - LANE + width
    shifted, scales = pl.pallas_call(
        functools.partial(prepare_kernel, length),
        out_shape=[
            jax.ShapeDtypeStruct((2, 2 * block_rows, used), BF16),
            jax.ShapeDtypeStruct((TURNS * block_rows, 2 * lags), BF16),
        ],
        in_specs=[vmem, vmem],
        out_specs=[vmem, vmem],
        scratch_shapes=[pltpu.VMEM((block_rows, total), F32)],
        name="prepare",
    )(prior, whole_time)

    half = group_size // 2
    kept, given = pl.pallas_call(
        functools.partial(correlate_kernel, length),
        out_shape=[jax.ShapeDtypeStruct((half, lags), F32)] * 2,
        in_specs=[vmem] * 3,
        out_specs=[vmem] * 2,
        scratch_shapes=[
            pltpu.VMEM((2, 2 * positions, used), BF16),
            pltpu.VMEM((positions, width), F32),
            pltpu.VMEM((positions, lags), F32),
            pltpu.VMEM((GROUP * STEP, width), BF16),
        ],
        compiler_params=pltpu.CompilerParams(vmem_limit_bytes=32 * 1024 * 1024),
        name="correlate",
    )(arrived, shifted, scales)

    distance = sta_size // 2
    while True:
        pairs = [(i, i ^ distance) for i in range(sta_size)]
        kept = kept + lax.ppermute(given, "sta", pairs)
        if distance == 1:
            return kept
        distance //= 2
        kept, given = kept[:distance], kept[distance:]


def solution(mesh):
    in_specs = (
        P("sta", "tpl"),
        P("sta", None),
        P("tpl", "sta", None),
        P("tpl", "sta"),
        P("tpl"),
        P(),
    )
    out_specs = P(("tpl", "sta"), None)
    return jax.shard_map(
        per_device, mesh=mesh, in_specs=in_specs, out_specs=out_specs, check_vma=False
    )
```

time: 335 us -> 42 us (0.13)
  matrix products: 246 us -> 0 us
  blocking collectives: 39.9 us -> 5.84 us
  other arithmetic: 15.9 us -> 0.61 us
  Pallas kernels: 0 us -> 13.4 us
  local copies, waits for them, and re-layouts: 14.2 us -> 2.22 us
    conv_general_dilated x1 -> x0, matrix products: 246 us -> none  [correlate(): lax.conv_general_dilated(data_rows[None], wave_rows[:, None, :], (1,), 'V...]
    unnamed x1 -> x0, blocking collectives: 34.5 us -> none
    another operation x4 -> x0, other arithmetic: 14 us -> none
    pallas_call x0 -> x3, Pallas kernels: none -> 13.4 us  [the longest x1 8.53 us: per_device(): pl.pallas_call(functools.partial(correlate_kernel, length), out_shape=[ja...]
    ppermute x0 -> x3, starting transfers between devices: none -> 7.11 us  [per_device(): kept = kept + lax.ppermute(given, 'sta', pairs)]
    gather x6 -> x0, local copies, waits for them, and re-layouts: 5.92 us -> none  [the longest x3 1.95 us: per_device(): traces = correlate(extended[wanted], arrived) * block_scales[wanted]]
    all_to_all x2 -> x1, starting transfers between devices: 13.3 us -> 7.41 us  [per_device(): lax.all_to_all(sent.reshape(sta_size, positions // sta_size, width), 'sta...]
    ppermute x0 -> x3, waiting for transfers between devices: none -> 4.98 us  [per_device(): kept = kept + lax.ppermute(given, 'sta', pairs)]
  transfers between devices with their start and end apart: 2 -> 4, of which waited for: 1 -> 3; matrix products, arithmetic and copies ran while one was open for 6% -> 0% of each run, Pallas kernels for 0% -> 6%
where the time goes in v1:
time: 42 us; the launch traced here: 41.6 us
  starting transfers between devices  14.5 us (35%)
  Pallas kernels  13.4 us (32%)
  blocking collectives  5.84 us (14%)
  waiting for transfers between devices  4.98 us (12%)
  local copies, waits for them, and re-layouts  2.22 us (5%)
  other arithmetic  0.61 us (1%)
    pallas_call x1, Pallas kernels, per_device(): pl.pallas_call(functools.partial(correlate_kernel, length), out_shape=[ja...  8.53 us
    all_to_all x1, starting transfers between devices, per_device(): lax.all_to_all(sent.reshape(sta_size, positions // sta_size, width), 'sta...  7.41 us
    ppermute x3, starting transfers between devices, per_device(): kept = kept + lax.ppermute(given, 'sta', pairs)  7.11 us
    all_gather x1, blocking collectives, per_device(): whole_time = lax.all_gather(window, 'tpl', axis=1, tiled=True)  5.84 us
    ppermute x3, waiting for transfers between devices, per_device(): kept = kept + lax.ppermute(given, 'sta', pairs)  4.98 us
    pallas_call x1, Pallas kernels, per_device(): pl.pallas_call(functools.partial(prepare_kernel, length), out_shape=[jax....  2.65 us
    pallas_call x1, Pallas kernels, per_device(): pl.pallas_call(functools.partial(route_kernel, sta_size, block_rows), out...  2.26 us
    unnamed x6, local copies, waits for them, and re-layouts  2.2 us
  transfers between devices with their start and end apart: 4, of which 3 were waited for; matrix products, arithmetic and copies ran while one was open for 0% of the time, Pallas kernels for 6%

profile of v1, /device:TPU:0, one launch (start us, length us, event | category | flops | bytes accessed | tf_op | source)
XLA Modules:
  0.0 41.6 jit_solution(5087970351122144809)
XLA Ops:
  0.0 2.3 %route.1 = bf16[128,640]{1,0:T(8,128)(2,1)} custom-call(s32[1]{0:T(128)} %bitcast.sta_pos, bf16[128,600]{1,0:T(8,128)(2,1)} %bitcast.7, s32[8,16]{1,0:T(8,128)} %chan_list.1, s32[8]{0:T(128)} %chan_count.1, s32[1,128]{1,0:T(1,128)} %bitcast.8), custom_call_target="tpu_custom_call" | custom-call | tf_op jit(solution)/shard_map/route/pallas_call | solution.py:218
  2.3 0.0 copy-start.2
  2.3 7.4 %all-to-all-start = ((bf16[8,16,640]{2,1,0:T(8,128)(2,1)}), bf16[8,16,640]{2,1,0:T(8,128)(2,1)S(1)}, u32[]{:S(2)}, u32[]{:S(2)}) async-start(bf16[8,16,640]{2,1,0:T(8,128)(2,1)} %bitcast.6), calls=%async_computation | async-start | bytes 327680 | tf_op jit(solution)/shard_map/all_to_all | solution.py:232
  9.7 0.0 copy-done.2
  9.7 5.8 %all_gather.3.window = bf16[48,1024]{1,0:T(8,128)(2,1)} all-gather(bf16[48,256]{1,0:T(8,128)(2,1)S(1)} %copy-done.2), channel_id=1, replica_groups=mesh['sta'=8,'tpl'=4] {'tpl'}, dimensions={1}, use_global_device_ids=true | all-gather | bytes 122880 | tf_op jit(solution)/shard_map/all_gather | solution.py:240
  15.5 2.7 %prepare.1 = (bf16[2,96,1536]{2,1,0:T(8,128)(2,1)}, bf16[192,2048]{1,0:T(8,128)(2,1)}) custom-call(bf16[48,599]{1,0:T(8,128)(2,1)} %prior.1, bf16[48,1024]{1,0:T(8,128)(2,1)} %all_gather.3.window), custom_call_target="tpu_custom_call" | custom-call | tf_op jit(solution)/shard_map/prepare/pallas_call | solution.py:243
  18.2 0.0 all-to-all-done
  18.2 0.0 copy-start
  18.2 1.1 %copy-done = bf16[192,2048]{1,0:T(8,128)(2,1)S(1)} copy-done((bf16[192,2048]{1,0:T(8,128)(2,1)S(1)}, bf16[192,2048]{1,0:T(8,128)(2,1)}, u32[]{:S(2)}) %copy-start) | copy-done | bytes 786456
  19.3 0.0 copy-start.1
  19.3 1.1 %copy-done.1 = bf16[2,96,1536]{2,1,0:T(8,128)(2,1)S(1)} copy-done((bf16[2,96,1536]{2,1,0:T(8,128)(2,1)S(1)}, bf16[2,96,1536]{2,1,0:T(8,128)(2,1)}, u32[]{:S(2)}) %copy-start.1) | copy-done | bytes 589848
  20.4 8.5 %correlate.1 = (f32[4,1024]{1,0:T(4,128)S(1)}, f32[4,1024]{1,0:T(4,128)S(1)}) custom-call(bf16[128,640]{1,0:T(8,128)(2,1)S(1)} %bitcast.5, bf16[2,96,1536]{2,1,0:T(8,128)(2,1)S(1)} %copy-done.1, bf16[192,2048]{1,0:T(8,128)(2,1)S(1)} %copy-done), custom_call_target="tpu_custom_call" | custom-call | tf_op jit(solution)/shard_map/correlate/pallas_call | solution.py:256
  28.9 3.0 %collective-permute-start = (f32[4,1024]{1,0:T(4,128)S(1)}, f32[4,1024]{1,0:T(4,128)S(1)}, u32[]{:S(2)}, u32[]{:S(2)}) collective-permute-start(f32[4,1024]{1,0:T(4,128)S(1)} %get-tuple-element.12), channel_id=1, source_target_pairs={{0,16},{4,20},{8,24},{12,28},{16,0},{20,4},{24,8},{28,12},{1,17},{... | collective-permute-start | bytes 49160 | tf_op jit(solution)/shard_map/ppermute | solution.py:274
  31.9 1.7 %collective-permute-done = f32[4,1024]{1,0:T(4,128)S(1)} collective-permute-done((f32[4,1024]{1,0:T(4,128)S(1)}, f32[4,1024]{1,0:T(4,128)S(1)}, u32[]{:S(2)}, u32[]{:S(2)}) %collective-permute-start) | collective-permute-done | bytes 16416 | tf_op jit(solution)/shard_map/ppermute | solution.py:274
  33.6 2.1 %collective-permute-start.1 = (f32[2,1024]{1,0:T(2,128)S(1)}, f32[2,1024]{1,0:T(2,128)S(1)}, u32[]{:S(2)}, u32[]{:S(2)}) collective-permute-start(f32[2,1024]{1,0:T(2,128)S(1)} %slice.17), channel_id=1, source_target_pairs={{0,8},{4,12},{8,0},{12,4},{16,24},{20,28},{24,16},{28,20},{1,9},{5... | collective-permute-start | bytes 24584 | tf_op jit(solution)/shard_map/ppermute | solution.py:274
  35.7 1.6 %collective-permute-done.1 = f32[2,1024]{1,0:T(2,128)S(1)} collective-permute-done((f32[2,1024]{1,0:T(2,128)S(1)}, f32[2,1024]{1,0:T(2,128)S(1)}, u32[]{:S(2)}, u32[]{:S(2)}) %collective-permute-start.1) | collective-permute-done | bytes 8224 | tf_op jit(solution)/shard_map/ppermute | solution.py:274
  37.4 2.1 %collective-permute-start.2 = (f32[1,1024]{1,0:T(1,128)S(1)}, f32[1,1024]{1,0:T(1,128)S(1)}, u32[]{:S(2)}, u32[]{:S(2)}) collective-permute-start(f32[1,1024]{1,0:T(1,128)S(1)} %slice.19), channel_id=1, source_target_pairs={{0,4},{4,0},{8,12},{12,8},{16,20},{20,16},{24,28},{28,24},{1,5},{5... | collective-permute-start | bytes 12296 | tf_op jit(solution)/shard_map/ppermute | solution.py:274
  39.4 1.6 %collective-permute-done.2 = f32[1,1024]{1,0:T(1,128)S(1)} collective-permute-done((f32[1,1024]{1,0:T(1,128)S(1)}, f32[1,1024]{1,0:T(1,128)S(1)}, u32[]{:S(2)}, u32[]{:S(2)}) %collective-permute-start.2) | collective-permute-done | bytes 4128 | tf_op jit(solution)/shard_map/ppermute | solution.py:274
  41.0 0.6 %slice_add_fusion.1 = f32[1,1024]{1,0:T(1,128)} fusion(f32[1,1024]{1,0:T(1,128)S(1)} %collective-permute-done.2, f32[2,1024]{1,0:T(2,128)S(1)} %slice_add_fusion), kind=kLoop, calls=%fused_computation.1 | loop fusion | flops 1024 | bytes 12288 | tf_op jit(solution)/shard_map/add | solution.py:274
  (4 shorter events, 0.0 us)
Async XLA Ops:
  2.3 7.4 %copy-start.2 = (bf16[48,256]{1,0:T(8,128)(2,1)S(1)}, bf16[48,256]{1,0:T(8,128)(2,1)}, u32[]{:S(2)}) copy-start(bf16[48,256]{1,0:T(8,128)(2,1)} %param.6) | copy-start | bytes 73732
  2.3 15.9 %all-to-all-start = ((bf16[8,16,640]{2,1,0:T(8,128)(2,1)}), bf16[8,16,640]{2,1,0:T(8,128)(2,1)S(1)}, u32[]{:S(2)}, u32[]{:S(2)}) async-start(bf16[8,16,640]{2,1,0:T(8,128)(2,1)} %bitcast.6), calls=%async_computation | async-start | bytes 327680 | tf_op jit(solution)/shard_map/all_to_all | solution.py:232
  18.2 1.1 %copy-start = (bf16[192,2048]{1,0:T(8,128)(2,1)S(1)}, bf16[192,2048]{1,0:T(8,128)(2,1)}, u32[]{:S(2)}) copy-start(bf16[192,2048]{1,0:T(8,128)(2,1)} %get-tuple-element.10.scales) | copy-start | bytes 2359300
  19.3 1.1 %copy-start.1 = (bf16[2,96,1536]{2,1,0:T(8,128)(2,1)S(1)}, bf16[2,96,1536]{2,1,0:T(8,128)(2,1)}, u32[]{:S(2)}) copy-start(bf16[2,96,1536]{2,1,0:T(8,128)(2,1)} %get-tuple-element.9.shifted) | copy-start | bytes 1769476
  28.9 4.7 %collective-permute-start = (f32[4,1024]{1,0:T(4,128)S(1)}, f32[4,1024]{1,0:T(4,128)S(1)}, u32[]{:S(2)}, u32[]{:S(2)}) collective-permute-start(f32[4,1024]{1,0:T(4,128)S(1)} %get-tuple-element.12), channel_id=1, source_target_pairs={{0,16},{4,20},{8,24},{12,28},{16,0},{20,4},{24,8},{28,12},{1,17},{... | collective-permute-start | bytes 49160 | tf_op jit(solution)/shard_map/ppermute | solution.py:274
  33.6 3.7 %collective-permute-start.1 = (f32[2,1024]{1,0:T(2,128)S(1)}, f32[2,1024]{1,0:T(2,128)S(1)}, u32[]{:S(2)}, u32[]{:S(2)}) collective-permute-start(f32[2,1024]{1,0:T(2,128)S(1)} %slice.17), channel_id=1, source_target_pairs={{0,8},{4,12},{8,0},{12,4},{16,24},{20,28},{24,16},{28,20},{1,9},{5... | collective-permute-start | bytes 24584 | tf_op jit(solution)/shard_map/ppermute | solution.py:274
  37.4 3.7 %collective-permute-start.2 = (f32[1,1024]{1,0:T(1,128)S(1)}, f32[1,1024]{1,0:T(1,128)S(1)}, u32[]{:S(2)}, u32[]{:S(2)}) collective-permute-start(f32[1,1024]{1,0:T(1,128)S(1)} %slice.19), channel_id=1, source_target_pairs={{0,4},{4,0},{8,12},{12,8},{16,20},{20,16},{24,28},{28,24},{1,5},{5... | collective-permute-start | bytes 12296 | tf_op jit(solution)/shard_map/ppermute | solution.py:274

commit v2 on v1

--- a/solution.py
+++ b/solution.py
@@ -12,6 +12,7 @@
 STEP = 32
 GROUP = 8
 TURNS = LANE // STEP
+MIB = 1 << 20
 F32, BF16, I32 = jnp.float32, jnp.bfloat16, jnp.int32
 
 
@@ -186,7 +187,7 @@
             traces[pl.ds(first, GROUP), at_lag] = traces[pl.ds(first, GROUP), at_lag] * own[a]
         return 0
 
-    lax.fori_loop(0, positions // GROUP, one_group, 0)
+    lax.fori_loop(0, positions // GROUP, one_group, 0, unroll=True)
     scaled = traces[...]
     high = scaled.astype(BF16)
     low = (scaled - high.astype(F32)).astype(BF16)
@@ -221,6 +222,7 @@
         in_specs=[smem, vmem, vmem, smem, vmem],
         out_specs=vmem,
         scratch_shapes=[pltpu.VMEM((positions, width), F32)],
+        compiler_params=pltpu.CompilerParams(vmem_limit_bytes=8 * MIB),
         name="route",
     )(
         sta_pos,
@@ -249,6 +251,7 @@
         in_specs=[vmem, vmem],
         out_specs=[vmem, vmem],
         scratch_shapes=[pltpu.VMEM((block_rows, total), F32)],
+        compiler_params=pltpu.CompilerParams(vmem_limit_bytes=16 * MIB),
         name="prepare",
     )(prior, whole_time)
 
@@ -264,7 +267,7 @@
             pltpu.VMEM((positions, lags), F32),
             pltpu.VMEM((GROUP * STEP, width), BF16),
         ],
-        compiler_params=pltpu.CompilerParams(vmem_limit_bytes=32 * 1024 * 1024),
+        compiler_params=pltpu.CompilerParams(vmem_limit_bytes=16 * MIB),
         name="correlate",
     )(arrived, shifted, scales)
 

time: 42 us -> 34.6 us (0.82)
  Pallas kernels: 13.4 us -> 5.8 us
  waiting for transfers between devices: 4.98 us -> 9.73 us
  starting transfers between devices: 14.5 us -> 11 us
  local copies, waits for them, and re-layouts: 2.22 us -> 1.63 us
    pallas_call x1, Pallas kernels: 8.53 us -> 3.1 us  [per_device(): pl.pallas_call(functools.partial(correlate_kernel, length), out_shape=[ja...]
    ppermute x3, starting transfers between devices: 7.11 us -> 3.59 us  [per_device(): kept = kept + lax.ppermute(given, 'sta', pairs)]
    ppermute x3, waiting for transfers between devices: 4.98 us -> 8.5 us  [per_device(): kept = kept + lax.ppermute(given, 'sta', pairs)]
    pallas_call x1, Pallas kernels: 2.65 us -> 0.84 us  [per_device(): pl.pallas_call(functools.partial(prepare_kernel, length), out_shape=[jax....]
    all_to_all x1, waiting for transfers between devices: 0.01 us -> 1.23 us  [per_device(): lax.all_to_all(sent.reshape(sta_size, positions // sta_size, width), 'sta...]
    unnamed x6 -> x12, local copies, waits for them, and re-layouts: 2.2 us -> 1.62 us
  transfers between devices with their start and end apart: 4 -> 4, of which waited for: 3 -> 4; matrix products, arithmetic and copies ran while one was open for 0% -> 0% of each run, Pallas kernels for 6% -> 2%
where the time goes in v2:
time: 34.6 us; the launch traced here: 34.3 us
  starting transfers between devices  11 us (32%)
  waiting for transfers between devices  9.73 us (28%)
  Pallas kernels  5.8 us (17%)
  blocking collectives  5.47 us (16%)
  local copies, waits for them, and re-layouts  1.63 us (5%)
  other arithmetic  0.61 us (2%)
    ppermute x3, waiting for transfers between devices, per_device(): kept = kept + lax.ppermute(given, 'sta', pairs)  8.5 us
    all_to_all x1, starting transfers between devices, per_device(): lax.all_to_all(sent.reshape(sta_size, positions // sta_size, width), 'sta...  7.41 us
    all_gather x1, blocking collectives, per_device(): whole_time = lax.all_gather(window, 'tpl', axis=1, tiled=True)  5.47 us
    ppermute x3, starting transfers between devices, per_device(): kept = kept + lax.ppermute(given, 'sta', pairs)  3.59 us
    pallas_call x1, Pallas kernels, per_device(): pl.pallas_call(functools.partial(correlate_kernel, length), out_shape=[ja...  3.1 us
    pallas_call x1, Pallas kernels, per_device(): pl.pallas_call(functools.partial(route_kernel, sta_size, block_rows), out...  1.87 us
    unnamed x12, local copies, waits for them, and re-layouts  1.62 us
    all_to_all x1, waiting for transfers between devices, per_device(): lax.all_to_all(sent.reshape(sta_size, positions // sta_size, width), 'sta...  1.23 us
  transfers between devices with their start and end apart: 4, of which 4 were waited for; matrix products, arithmetic and copies ran while one was open for 0% of the time, Pallas kernels for 2%

profile of v2, /device:TPU:0, one launch (start us, length us, event | category | flops | bytes accessed | tf_op | source)
XLA Modules:
  0.0 34.3 jit_solution(8138982193726595437)
XLA Ops:
  0.0 0.0 copy-start.2
  0.0 0.0 copy-start.3
  0.0 0.0 copy-start.4
  0.0 0.7 %copy-done.2 = s32[8,16]{1,0:T(8,128)S(1)} copy-done((s32[8,16]{1,0:T(8,128)S(1)}, s32[8,16]{1,0:T(8,128)}, u32[]{:S(2)}) %copy-start.2) | copy-done | bytes 536
  0.7 0.0 copy-done.3
  0.7 0.0 copy-done.4
  0.7 0.0 copy-start
  0.7 0.9 %copy-done = bf16[8,16,600]{2,1,0:T(8,128)(2,1)S(1)} copy-done((bf16[8,16,600]{2,1,0:T(8,128)(2,1)S(1)}, bf16[8,16,600]{2,1,0:T(8,128)(2,1)}, u32[]{:S(2)}) %copy-start) | copy-done | bytes 153624
  1.6 1.9 %route.1 = bf16[128,640]{1,0:T(8,128)(2,1)} custom-call(s32[1]{0:T(128)} %bitcast.sta_pos, bf16[128,600]{1,0:T(8,128)(2,1)S(1)} %bitcast.6, s32[8,16]{1,0:T(8,128)S(1)} %copy-done.2, s32[8]{0:T(128)S(1)} %copy-done.3, s32[1,128]{1,0:T(1,128)S(1)} %bitcast.7), custom_call_target="tpu_custom_call" | custom-call | tf_op jit(solution)/shard_map/route/pallas_call | solution.py:219
  3.5 0.0 copy-start.5
  3.5 7.4 %all-to-all-start = ((bf16[8,16,640]{2,1,0:T(8,128)(2,1)}), bf16[8,16,640]{2,1,0:T(8,128)(2,1)S(1)}, u32[]{:S(2)}, u32[]{:S(2)}) async-start(bf16[8,16,640]{2,1,0:T(8,128)(2,1)} %bitcast.3), calls=%async_computation | async-start | bytes 327680 | tf_op jit(solution)/shard_map/all_to_all | solution.py:234
  10.9 0.0 copy-done.5
  10.9 0.0 copy-start.1
  10.9 5.5 %all_gather.3.window = bf16[48,1024]{1,0:T(8,128)(2,1)S(1)} all-gather(bf16[48,256]{1,0:T(8,128)(2,1)S(1)} %copy-done.5), channel_id=1, replica_groups=mesh['sta'=8,'tpl'=4] {'tpl'}, dimensions={1}, use_global_device_ids=true | all-gather | bytes 122880 | tf_op jit(solution)/shard_map/all_gather | solution.py:242
  16.4 0.0 copy-done.1
  16.4 0.8 %prepare.1 = (bf16[2,96,1536]{2,1,0:T(8,128)(2,1)S(1)}, bf16[192,2048]{1,0:T(8,128)(2,1)S(1)}) custom-call(bf16[48,599]{1,0:T(8,128)(2,1)S(1)} %copy-done.1, bf16[48,1024]{1,0:T(8,128)(2,1)S(1)} %all_gather.3.window), custom_call_target="tpu_custom_call" | custom-call | tf_op jit(solution)/shard_map/prepare/pallas_call | solution.py:245
  17.2 1.2 %all-to-all-done = bf16[8,16,640]{2,1,0:T(8,128)(2,1)S(1)} async-done(((bf16[8,16,640]{2,1,0:T(8,128)(2,1)}), bf16[8,16,640]{2,1,0:T(8,128)(2,1)S(1)}, u32[]{:S(2)}, u32[]{:S(2)}) %all-to-all-start) | async-done | bytes 163872 | tf_op jit(solution)/shard_map/all_to_all | solution.py:234
  18.5 3.1 %correlate.1 = (f32[4,1024]{1,0:T(4,128)S(1)}, f32[4,1024]{1,0:T(4,128)S(1)}) custom-call(bf16[128,640]{1,0:T(8,128)(2,1)S(1)} %bitcast.5, bf16[2,96,1536]{2,1,0:T(8,128)(2,1)S(1)} %get-tuple-element.9.shifted, bf16[192,2048]{1,0:T(8,128)(2,1)S(1)} %get-tuple-element.10.scales), custom_call_target="tpu_custom_call" | custom-call | tf_op jit(solution)/shard_map/correlate/pallas_call | solution.py:259
  21.6 1.8 %collective-permute-start = (f32[4,1024]{1,0:T(4,128)S(1)}, f32[4,1024]{1,0:T(4,128)S(1)}, u32[]{:S(2)}, u32[]{:S(2)}) collective-permute-start(f32[4,1024]{1,0:T(4,128)S(1)} %get-tuple-element.12), channel_id=1, source_target_pairs={{0,16},{4,20},{8,24},{12,28},{16,0},{20,4},{24,8},{28,12},{1,17},{... | collective-permute-start | bytes 49160 | tf_op jit(solution)/shard_map/ppermute | solution.py:277
  23.3 2.9 %collective-permute-done = f32[4,1024]{1,0:T(4,128)S(1)} collective-permute-done((f32[4,1024]{1,0:T(4,128)S(1)}, f32[4,1024]{1,0:T(4,128)S(1)}, u32[]{:S(2)}, u32[]{:S(2)}) %collective-permute-start) | collective-permute-done | bytes 16416 | tf_op jit(solution)/shard_map/ppermute | solution.py:277
  26.3 0.9 %collective-permute-start.1 = (f32[2,1024]{1,0:T(2,128)S(1)}, f32[2,1024]{1,0:T(2,128)S(1)}, u32[]{:S(2)}, u32[]{:S(2)}) collective-permute-start(f32[2,1024]{1,0:T(2,128)S(1)} %slice.17), channel_id=1, source_target_pairs={{0,8},{4,12},{8,0},{12,4},{16,24},{20,28},{24,16},{28,20},{1,9},{5... | collective-permute-start | bytes 24584 | tf_op jit(solution)/shard_map/ppermute | solution.py:277
  27.1 2.9 %collective-permute-done.1 = f32[2,1024]{1,0:T(2,128)S(1)} collective-permute-done((f32[2,1024]{1,0:T(2,128)S(1)}, f32[2,1024]{1,0:T(2,128)S(1)}, u32[]{:S(2)}, u32[]{:S(2)}) %collective-permute-start.1) | collective-permute-done | bytes 8224 | tf_op jit(solution)/shard_map/ppermute | solution.py:277
  30.0 1.0 %collective-permute-start.2 = (f32[1,1024]{1,0:T(1,128)S(1)}, f32[1,1024]{1,0:T(1,128)S(1)}, u32[]{:S(2)}, u32[]{:S(2)}) collective-permute-start(f32[1,1024]{1,0:T(1,128)S(1)} %slice.19), channel_id=1, source_target_pairs={{0,4},{4,0},{8,12},{12,8},{16,20},{20,16},{24,28},{28,24},{1,5},{5... | collective-permute-start | bytes 12296 | tf_op jit(solution)/shard_map/ppermute | solution.py:277
  31.0 2.7 %collective-permute-done.2 = f32[1,1024]{1,0:T(1,128)S(1)} collective-permute-done((f32[1,1024]{1,0:T(1,128)S(1)}, f32[1,1024]{1,0:T(1,128)S(1)}, u32[]{:S(2)}, u32[]{:S(2)}) %collective-permute-start.2) | collective-permute-done | bytes 4128 | tf_op jit(solution)/shard_map/ppermute | solution.py:277
  33.7 0.6 %slice_add_fusion.1 = f32[1,1024]{1,0:T(1,128)} fusion(f32[1,1024]{1,0:T(1,128)S(1)} %collective-permute-done.2, f32[2,1024]{1,0:T(2,128)S(1)} %slice_add_fusion), kind=kLoop, calls=%fused_computation.1 | loop fusion | flops 1024 | bytes 12288 | tf_op jit(solution)/shard_map/add | solution.py:277
  (4 shorter events, 0.0 us)
Async XLA Ops:
  0.0 0.7 %copy-start.2 = (s32[8,16]{1,0:T(8,128)S(1)}, s32[8,16]{1,0:T(8,128)}, u32[]{:S(2)}) copy-start(s32[8,16]{1,0:T(8,128)} %chan_list.1) | copy-start | bytes 1540
  0.0 0.7 %copy-start.3 = (s32[8]{0:T(128)S(1)}, s32[8]{0:T(128)}, u32[]{:S(2)}) copy-start(s32[8]{0:T(128)} %chan_count.1) | copy-start | bytes 100
  0.0 0.7 %copy-start.4 = (s32[128]{0:T(128)S(1)}, s32[128]{0:T(128)}, u32[]{:S(2)}) copy-start(s32[128]{0:T(128)} %param.11) | copy-start | bytes 1540
  0.7 0.9 %copy-start = (bf16[8,16,600]{2,1,0:T(8,128)(2,1)S(1)}, bf16[8,16,600]{2,1,0:T(8,128)(2,1)}, u32[]{:S(2)}) copy-start(bf16[8,16,600]{2,1,0:T(8,128)(2,1)} %param.8) | copy-start | bytes 460804
  3.5 7.4 %copy-start.5 = (bf16[48,256]{1,0:T(8,128)(2,1)S(1)}, bf16[48,256]{1,0:T(8,128)(2,1)}, u32[]{:S(2)}) copy-start(bf16[48,256]{1,0:T(8,128)(2,1)} %param.6) | copy-start | bytes 73732
  3.5 15.0 %all-to-all-start = ((bf16[8,16,640]{2,1,0:T(8,128)(2,1)}), bf16[8,16,640]{2,1,0:T(8,128)(2,1)S(1)}, u32[]{:S(2)}, u32[]{:S(2)}) async-start(bf16[8,16,640]{2,1,0:T(8,128)(2,1)} %bitcast.3), calls=%async_computation | async-start | bytes 327680 | tf_op jit(solution)/shard_map/all_to_all | solution.py:234
  10.9 5.5 %copy-start.1 = (bf16[48,599]{1,0:T(8,128)(2,1)S(1)}, bf16[48,599]{1,0:T(8,128)(2,1)}, u32[]{:S(2)}) copy-start(bf16[48,599]{1,0:T(8,128)(2,1)} %prior.1) | copy-start | bytes 172516
  21.6 4.7 %collective-permute-start = (f32[4,1024]{1,0:T(4,128)S(1)}, f32[4,1024]{1,0:T(4,128)S(1)}, u32[]{:S(2)}, u32[]{:S(2)}) collective-permute-start(f32[4,1024]{1,0:T(4,128)S(1)} %get-tuple-element.12), channel_id=1, source_target_pairs={{0,16},{4,20},{8,24},{12,28},{16,0},{20,4},{24,8},{28,12},{1,17},{... | collective-permute-start | bytes 49160 | tf_op jit(solution)/shard_map/ppermute | solution.py:277
  26.3 3.7 %collective-permute-start.1 = (f32[2,1024]{1,0:T(2,128)S(1)}, f32[2,1024]{1,0:T(2,128)S(1)}, u32[]{:S(2)}, u32[]{:S(2)}) collective-permute-start(f32[2,1024]{1,0:T(2,128)S(1)} %slice.17), channel_id=1, source_target_pairs={{0,8},{4,12},{8,0},{12,4},{16,24},{20,28},{24,16},{28,20},{1,9},{5... | collective-permute-start | bytes 24584 | tf_op jit(solution)/shard_map/ppermute | solution.py:277
  30.0 3.7 %collective-permute-start.2 = (f32[1,1024]{1,0:T(1,128)S(1)}, f32[1,1024]{1,0:T(1,128)S(1)}, u32[]{:S(2)}, u32[]{:S(2)}) collective-permute-start(f32[1,1024]{1,0:T(1,128)S(1)} %slice.19), channel_id=1, source_target_pairs={{0,4},{4,0},{8,12},{12,8},{16,20},{20,16},{24,28},{28,24},{1,5},{5... | collective-permute-start | bytes 12296 | tf_op jit(solution)/shard_map/ppermute | solution.py:277

commit v3 on v2

v3 whole, which is shorter than its diff:
```python
import functools

import jax
import jax.numpy as jnp
from jax import lax
from jax.experimental import pallas as pl
from jax.experimental.pallas import tpu as pltpu
from jax.sharding import PartitionSpec as P

epsilon = 1e-06
LANE = 128
STEP = 32
GROUP = 8
CHUNK = 1
TURNS = LANE // STEP
MIB = 1 << 20
F32, BF16, I32 = jnp.float32, jnp.bfloat16, jnp.int32


def up(value, unit):
    return -(-value // unit) * unit


def column_sum(values):
    return jnp.sum(values, axis=1, keepdims=True)


def route_kernel(
    sta_size,
    block_rows,
    sta_pos,
    waves_in,
    chan_list_in,
    chan_count_in,
    station_row_in,
    sent,
    waves,
    chan_list,
    chan_count,
    station_row,
    channels,
    padded,
    arrivals,
):
    copies = [
        pltpu.make_async_copy(source, target, arrivals.at[i])
        for i, (source, target) in enumerate(
            (
                (chan_list_in, chan_list),
                (station_row_in, station_row),
                (chan_count_in, chan_count),
                (waves_in, waves),
            )
        )
    ]
    for copy in copies:
        copy.start()
    positions, length = waves.shape
    group_size, slot_count = chan_list.shape
    width = sent.shape[1]
    capacity = positions // sta_size
    padded[:, width - LANE :] = jnp.zeros((positions, LANE), F32)
    channels[...] = jnp.zeros(channels.shape, I32)
    row = lax.broadcasted_iota(I32, (positions, positions), 0)
    lane = lax.broadcasted_iota(I32, (positions, positions), 1)
    before = (row < lane).astype(F32).astype(BF16)
    spot = lax.broadcasted_iota(I32, (positions, 1), 0)
    slot = sta_pos[0] * slot_count + spot % slot_count
    along = lax.broadcasted_iota(I32, (1, positions), 1)
    for copy in copies[:3]:
        copy.wait()

    channels[:, :slot_count] = chan_list[...]
    channel = channels[...]
    station = (channel * 21846) >> 16
    found = jnp.zeros(channel.shape, I32)
    for first in range(0, station_row.shape[1], LANE):
        some = jnp.broadcast_to(station_row[:, first : first + LANE], channel.shape)
        place = jnp.clip(station - first, 0, LANE - 1)
        here = (station >= first) & (station < first + LANE)
        found = jnp.where(here, jnp.take_along_axis(some, place, axis=1), found)
    data_row = 3 * found + channel - 3 * station
    spread = jnp.where(lax.broadcasted_iota(I32, channel.shape, 1) < slot_count, data_row, 0)
    spread = pltpu.roll(spread.astype(F32), 0, axis=1, stride=slot_count, stride_axis=0)
    data_row = jnp.sum(spread, axis=0, keepdims=True).astype(I32)
    owner = jnp.zeros((1, positions), I32)
    for o in range(1, sta_size):
        owner = owner + (data_row >= o * block_rows).astype(I32)
    local_row = data_row - owner * block_rows
    relative = along // slot_count ^ owner
    hits = (lax.broadcasted_iota(I32, (sta_size, positions), 0) == owner).astype(F32)
    ahead = jnp.dot(hits.astype(BF16), before, preferred_element_type=F32)
    rank = jnp.sum(ahead * hits, axis=0, keepdims=True).astype(I32)
    goes = row == owner * capacity + rank
    row_tag = column_sum(jnp.where(goes, local_row, 0).astype(F32))
    template_tag = column_sum(jnp.where(goes, relative, 0).astype(F32))

    count = jnp.zeros((positions, 1), I32)
    for t in range(group_size):
        count = jnp.where(spot // slot_count == t, chan_count[t], count)
    copies[3].wait()
    padded[:, :length] = waves[...].astype(F32)
    raw = padded[...]
    listed = (slot < count).astype(F32)
    gain = listed / jnp.sqrt(column_sum(raw * raw) + epsilon)
    ordered = jnp.dot(
        goes.astype(F32).astype(BF16), (raw * gain).astype(BF16), preferred_element_type=F32
    )
    wide = lax.broadcasted_iota(I32, (positions, width), 1)
    sent[...] = jnp.where(
        wide == length, row_tag, jnp.where(wide == length + 1, template_tag, ordered)
    ).astype(BF16)


def prepare_kernel(length, prior, window, shifted, scales, extended):
    rows, before = prior.shape
    lags = window.shape[1]
    total = extended.shape[1]
    start = before // LANE * LANE
    extended[:, :start] = jnp.zeros((rows, start), F32)
    extended[:, start:] = jnp.zeros((rows, total - start), F32)
    extended[:, start : start + lags] = window[...].astype(F32)
    moved = pltpu.roll(extended[:, start:], before - start, axis=1)
    extended[:, start:] = jnp.zeros((rows, total - start), F32)
    extended[:, :before] = prior[...].astype(F32)
    extended[:, start:] = extended[:, start:] + moved
    whole = extended[...]
    used = shifted.shape[1]
    for turn in range(TURNS):
        moved = whole if turn == 0 else pltpu.roll(whole, total - turn * STEP, axis=1)
        shifted[turn * rows : (turn + 1) * rows, :] = moved[:, :used].astype(BF16)
    square = whole * whole
    high = square.astype(BF16)
    low = (square - high.astype(F32)).astype(BF16)
    span = up(length + LANE - 1, LANE)
    sample = lax.broadcasted_iota(I32, (span, LANE), 0)
    lag = lax.broadcasted_iota(I32, (span, LANE), 1)
    band = ((sample >= lag) & (sample < lag + length)).astype(F32).astype(BF16)
    for a in range(lags // LANE):
        at = slice(a * LANE, a * LANE + span)
        energy = jnp.dot(high[:, at], band, preferred_element_type=F32) + jnp.dot(
            low[:, at], band, preferred_element_type=F32
        )
        scale = 1.0 / jnp.sqrt(energy + epsilon)
        scale_high = scale.astype(BF16)
        scales[:rows, a * LANE : (a + 1) * LANE] = scale_high
        scales[rows:, a * LANE : (a + 1) * LANE] = (scale - scale_high.astype(F32)).astype(BF16)


def correlate_kernel(
    length, arrived, shifted, scales, kept, given, frames, waves, traces, toeplitz, sums
):
    positions, width = arrived.shape
    rows = scales.shape[0] // 2
    lags = scales.shape[1]
    half = kept.shape[0]
    blocks = lags // LANE
    waves[...] = arrived[...].astype(F32)
    wanted = waves[:, length : length + 1].astype(I32)
    template = jnp.broadcast_to(waves[:, length + 1 : length + 2].astype(I32), (positions, LANE))

    pairs = wanted.reshape(positions // GROUP, 1, GROUP, 1)
    twice = jnp.concatenate([pairs, pairs], axis=1).reshape(2 * positions, 1)
    place = lax.broadcasted_iota(I32, (2 * positions, 1), 0)
    moved = place // GROUP % 2 + place % GROUP
    every = lax.broadcasted_iota(I32, (2 * positions, TURNS * rows), 1)
    for q in range(2):
        picks = every == (2 * q + moved) % TURNS * rows + twice
        frames[q] = jnp.dot(
            picks.astype(F32).astype(BF16), shifted[...], preferred_element_type=F32
        ).astype(BF16)
    either = lax.broadcasted_iota(I32, (positions, 2 * rows), 1)
    picks = (either == wanted) | (either == wanted + rows)
    picks = picks.astype(F32).astype(BF16)
    waves[:, width - LANE :] = jnp.where(
        lax.broadcasted_iota(I32, (positions, LANE), 1) < length - (width - LANE),
        waves[:, width - LANE :],
        0.0,
    )
    shape = (blocks * GROUP, LANE)
    member = lax.broadcasted_iota(I32, shape, 0) % GROUP
    low_half = member < TURNS
    turn = (lax.broadcasted_iota(I32, shape, 1) // STEP + 2 * TURNS - member) % TURNS

    for g in range(positions // GROUP):
        first = g * GROUP
        copies = toeplitz.at[g % toeplitz.shape[0]]
        for j in range(GROUP):
            wave = jnp.broadcast_to(waves[first + j : first + j + 1, :], (STEP, width))
            copies[j * STEP : (j + 1) * STEP, :] = pltpu.roll(
                wave, 0, axis=1, stride=1, stride_axis=0
            ).astype(BF16)
        at = slice(g * 2 * GROUP, (g + 1) * 2 * GROUP)
        data = [
            frames[q, at, a * LANE : a * LANE + width] for q in range(2) for a in range(blocks)
        ]
        product = lax.dot_general(
            jnp.concatenate(data, axis=0),
            copies[...],
            (((1,), (1,)), ((), ())),
            preferred_element_type=F32,
        )
        if g == 0:
            traces[...] = jnp.dot(picks, scales[...], preferred_element_type=F32)
        product = product.reshape(2, blocks, 2, GROUP, 2 * LANE)
        own = jnp.zeros(shape, F32)
        for step in range(TURNS):
            part = product[step // 2, :, step % 2].reshape(blocks * GROUP, 2 * LANE)
            part = jnp.where(low_half, part[:, :LANE], part[:, LANE:])
            if step > 0:
                part = pltpu.roll(part, step * STEP, axis=1)
            own = jnp.where(turn == step, part, own)
        own = own.reshape(blocks, GROUP, LANE)
        for a in range(blocks):
            at_lag = slice(a * LANE, (a + 1) * LANE)
            traces[first : first + GROUP, at_lag] = traces[first : first + GROUP, at_lag] * own[a]
        if (g + 1) % CHUNK == 0:
            for t in range(2 * half):
                total = jnp.zeros((GROUP, lags), F32) if g + 1 == CHUNK else sums[t]
                for done in range(g + 1 - CHUNK, g + 1):
                    ready = slice(done * GROUP, (done + 1) * GROUP)
                    mine = (template[ready] == t).astype(F32)
                    total = total + traces[ready, :] * jnp.concatenate([mine] * blocks, axis=1)
                sums[t] = total
    stacked = jnp.sum(sums[...], axis=1)
    kept[...] = stacked[:half]
    given[...] = stacked[half:]


def per_device(window, prior, waves, chan_list, chan_count, station_row):
    sta_size = lax.axis_size("sta")
    sta_pos = lax.axis_index("sta").astype(I32).reshape(1)
    group_size, slot_count, length = waves.shape
    positions = group_size * slot_count
    block_rows = prior.shape[0]
    width = up(length + STEP, LANE)
    lags = window.shape[1] * lax.axis_size("tpl")
    vmem = pl.BlockSpec(memory_space=pltpu.VMEM)
    smem = pl.BlockSpec(memory_space=pltpu.SMEM)

    anywhere = pl.BlockSpec(memory_space=pl.ANY)
    sent = pl.pallas_call(
        functools.partial(route_kernel, sta_size, block_rows),
        out_shape=jax.ShapeDtypeStruct((positions, width), BF16),
        in_specs=[smem] + [anywhere] * 4,
        out_specs=vmem,
        scratch_shapes=[
            pltpu.VMEM((positions, length), BF16),
            pltpu.VMEM((group_size, slot_count), I32),
            pltpu.SMEM((group_size,), I32),
            pltpu.VMEM((1, station_row.shape[0]), I32),
            pltpu.VMEM((group_size, LANE), I32),
            pltpu.VMEM((positions, width), F32),
            pltpu.SemaphoreType.DMA((4,)),
        ],
        name="route",
    )(
        sta_pos,
        waves.reshape(positions, length),
        chan_list,
        chan_count,
        station_row.reshape(1, station_row.shape[0]),
    )
    arrived = lax.all_to_all(
        sent.reshape(sta_size, positions // sta_size, width),
        "sta",
        split_axis=0,
        concat_axis=0,
        tiled=True,
    ).reshape(positions, width)

    whole_time = lax.all_gather(window, "tpl", axis=1, tiled=True)
    total = up(prior.shape[1] + lags, LANE)
    used = lags - LANE + width
    shifted, scales = pl.pallas_call(
        functools.partial(prepare_kernel, length),
        out_shape=[
            jax.ShapeDtypeStruct((TURNS * block_rows, used), BF16),
            jax.ShapeDtypeStruct((2 * block_rows, lags), BF16),
        ],
        in_specs=[vmem, vmem],
        out_specs=[vmem, vmem],
        scratch_shapes=[pltpu.VMEM((block_rows, total), F32)],
        compiler_params=pltpu.CompilerParams(vmem_limit_bytes=16 * MIB),
        name="prepare",
    )(prior, whole_time)

    half = group_size // 2
    kept, given = pl.pallas_call(
        functools.partial(correlate_kernel, length),
        out_shape=[jax.ShapeDtypeStruct((half, lags), F32)] * 2,
        in_specs=[vmem] * 3,
        out_specs=[vmem] * 2,
        scratch_shapes=[
            pltpu.VMEM((2, 2 * positions, used), BF16),
            pltpu.VMEM((positions, width), F32),
            pltpu.VMEM((positions, lags), F32),
            pltpu.VMEM((positions // GROUP, GROUP * STEP, width), BF16),
            pltpu.VMEM((group_size, GROUP, lags), F32),
        ],
        compiler_params=pltpu.CompilerParams(vmem_limit_bytes=16 * MIB),
        name="correlate",
    )(arrived, shifted, scales)

    distance = sta_size // 2
    while True:
        pairs = [(i, i ^ distance) for i in range(sta_size)]
        kept = kept + lax.ppermute(given, "sta", pairs)
        if distance == 1:
            return kept
        distance //= 2
        kept, given = kept[:distance], kept[distance:]


def solution(mesh):
    in_specs = (
        P("sta", "tpl"),
        P("sta", None),
        P("tpl", "sta", None),
        P("tpl", "sta"),
        P("tpl"),
        P(),
    )
    out_specs = P(("tpl", "sta"), None)
    return jax.shard_map(
        per_device, mesh=mesh, in_specs=in_specs, out_specs=out_specs, check_vma=False
    )
```

time: 34.6 us -> 32.9 us (0.951)
  local copies, waits for them, and re-layouts: 1.63 us -> 0.03 us
    unnamed x12 -> x4, local copies, waits for them, and re-layouts: 1.62 us -> 0.01 us
    pallas_call x1, Pallas kernels: 3.1 us -> 2.73 us  [per_device(): pl.pallas_call(functools.partial(correlate_kernel, length), out_shape=[ja...]
    pallas_call x1, Pallas kernels: 1.87 us -> 2.21 us  [per_device(): pl.pallas_call(functools.partial(route_kernel, sta_size, block_rows), out...]
where the time goes in v3:
time: 32.9 us; the launch traced here: 32.6 us
  starting transfers between devices  10.9 us (33%)
  waiting for transfers between devices  9.83 us (30%)
  Pallas kernels  5.69 us (17%)
  blocking collectives  5.47 us (17%)
  other arithmetic  0.61 us (2%)
    ppermute x3, waiting for transfers between devices, per_device(): kept = kept + lax.ppermute(given, 'sta', pairs)  8.51 us
    all_to_all x1, starting transfers between devices, per_device(): lax.all_to_all(sent.reshape(sta_size, positions // sta_size, width), 'sta...  7.3 us
    all_gather x1, blocking collectives, per_device(): whole_time = lax.all_gather(window, 'tpl', axis=1, tiled=True)  5.47 us
    ppermute x3, starting transfers between devices, per_device(): kept = kept + lax.ppermute(given, 'sta', pairs)  3.59 us
    pallas_call x1, Pallas kernels, per_device(): pl.pallas_call(functools.partial(correlate_kernel, length), out_shape=[ja...  2.73 us
    pallas_call x1, Pallas kernels, per_device(): pl.pallas_call(functools.partial(route_kernel, sta_size, block_rows), out...  2.21 us
    all_to_all x1, waiting for transfers between devices, per_device(): lax.all_to_all(sent.reshape(sta_size, positions // sta_size, width), 'sta...  1.32 us
    pallas_call x1, Pallas kernels, per_device(): pl.pallas_call(functools.partial(prepare_kernel, length), out_shape=[jax....  0.75 us
  transfers between devices with their start and end apart: 4, of which 4 were waited for; matrix products, arithmetic and copies ran while one was open for 0% of the time, Pallas kernels for 2%

profile of v3, /device:TPU:0, one launch (start us, length us, event | category | flops | bytes accessed | tf_op | source)
XLA Modules:
  0.0 32.6 jit_solution(8925427993865024501)
XLA Ops:
  0.0 2.2 %route.1 = bf16[128,640]{1,0:T(8,128)(2,1)} custom-call(s32[1]{0:T(128)} %bitcast.sta_pos, bf16[128,600]{1,0:T(8,128)(2,1)} %bitcast.7, s32[8,16]{1,0:T(8,128)} %chan_list_in.1, s32[8]{0:T(128)} %chan_count_in.1, s32[1,128]{1,0:T(1,128)} %bitcast.8), custom_call_target="tpu_custom_call" | custom-call | tf_op jit(solution)/shard_map/route/pallas_call | solution.py:242
  2.2 0.0 copy-start.1
  2.2 7.3 %all-to-all-start = ((bf16[8,16,640]{2,1,0:T(8,128)(2,1)}), bf16[8,16,640]{2,1,0:T(8,128)(2,1)S(1)}, u32[]{:S(2)}, u32[]{:S(2)}) async-start(bf16[8,16,640]{2,1,0:T(8,128)(2,1)} %bitcast.6), calls=%async_computation | async-start | bytes 327680 | tf_op jit(solution)/shard_map/all_to_all | solution.py:264
  9.5 0.0 copy-done.1
  9.5 0.0 copy-start
  9.5 5.5 %all_gather.3.window = bf16[48,1024]{1,0:T(8,128)(2,1)S(1)} all-gather(bf16[48,256]{1,0:T(8,128)(2,1)S(1)} %copy-done.1), channel_id=1, replica_groups=mesh['sta'=8,'tpl'=4] {'tpl'}, dimensions={1}, use_global_device_ids=true | all-gather | bytes 122880 | tf_op jit(solution)/shard_map/all_gather | solution.py:272
  15.0 0.0 copy-done
  15.0 0.8 %prepare.1 = (bf16[192,1536]{1,0:T(8,128)(2,1)S(1)}, bf16[96,1024]{1,0:T(8,128)(2,1)S(1)}) custom-call(bf16[48,599]{1,0:T(8,128)(2,1)S(1)} %copy-done, bf16[48,1024]{1,0:T(8,128)(2,1)S(1)} %all_gather.3.window), custom_call_target="tpu_custom_call" | custom-call | tf_op jit(solution)/shard_map/prepare/pallas_call | solution.py:275
  15.8 1.3 %all-to-all-done = bf16[8,16,640]{2,1,0:T(8,128)(2,1)S(1)} async-done(((bf16[8,16,640]{2,1,0:T(8,128)(2,1)}), bf16[8,16,640]{2,1,0:T(8,128)(2,1)S(1)}, u32[]{:S(2)}, u32[]{:S(2)}) %all-to-all-start) | async-done | bytes 163872 | tf_op jit(solution)/shard_map/all_to_all | solution.py:264
  17.1 2.7 %correlate.1 = (f32[4,1024]{1,0:T(4,128)S(1)}, f32[4,1024]{1,0:T(4,128)S(1)}) custom-call(bf16[128,640]{1,0:T(8,128)(2,1)S(1)} %bitcast.5, bf16[192,1536]{1,0:T(8,128)(2,1)S(1)} %get-tuple-element.9.shifted, bf16[96,1024]{1,0:T(8,128)(2,1)S(1)} %get-tuple-element.10.scales), custom_call_target="tpu_custom_call" | custom-call | tf_op jit(solution)/shard_map/correlate/pallas_call | solution.py:289
  19.8 1.7 %collective-permute-start = (f32[4,1024]{1,0:T(4,128)S(1)}, f32[4,1024]{1,0:T(4,128)S(1)}, u32[]{:S(2)}, u32[]{:S(2)}) collective-permute-start(f32[4,1024]{1,0:T(4,128)S(1)} %get-tuple-element.12), channel_id=1, source_target_pairs={{0,16},{4,20},{8,24},{12,28},{16,0},{20,4},{24,8},{28,12},{1,17},{... | collective-permute-start | bytes 49160 | tf_op jit(solution)/shard_map/ppermute | solution.py:308
  21.5 3.1 %collective-permute-done = f32[4,1024]{1,0:T(4,128)S(1)} collective-permute-done((f32[4,1024]{1,0:T(4,128)S(1)}, f32[4,1024]{1,0:T(4,128)S(1)}, u32[]{:S(2)}, u32[]{:S(2)}) %collective-permute-start) | collective-permute-done | bytes 16416 | tf_op jit(solution)/shard_map/ppermute | solution.py:308
  24.6 0.8 %collective-permute-start.1 = (f32[2,1024]{1,0:T(2,128)S(1)}, f32[2,1024]{1,0:T(2,128)S(1)}, u32[]{:S(2)}, u32[]{:S(2)}) collective-permute-start(f32[2,1024]{1,0:T(2,128)S(1)} %slice.17), channel_id=1, source_target_pairs={{0,8},{4,12},{8,0},{12,4},{16,24},{20,28},{24,16},{28,20},{1,9},{5... | collective-permute-start | bytes 24584 | tf_op jit(solution)/shard_map/ppermute | solution.py:308
  25.4 2.9 %collective-permute-done.1 = f32[2,1024]{1,0:T(2,128)S(1)} collective-permute-done((f32[2,1024]{1,0:T(2,128)S(1)}, f32[2,1024]{1,0:T(2,128)S(1)}, u32[]{:S(2)}, u32[]{:S(2)}) %collective-permute-start.1) | collective-permute-done | bytes 8224 | tf_op jit(solution)/shard_map/ppermute | solution.py:308
  28.3 1.1 %collective-permute-start.2 = (f32[1,1024]{1,0:T(1,128)S(1)}, f32[1,1024]{1,0:T(1,128)S(1)}, u32[]{:S(2)}, u32[]{:S(2)}) collective-permute-start(f32[1,1024]{1,0:T(1,128)S(1)} %slice.19), channel_id=1, source_target_pairs={{0,4},{4,0},{8,12},{12,8},{16,20},{20,16},{24,28},{28,24},{1,5},{5... | collective-permute-start | bytes 12296 | tf_op jit(solution)/shard_map/ppermute | solution.py:308
  29.4 2.5 %collective-permute-done.2 = f32[1,1024]{1,0:T(1,128)S(1)} collective-permute-done((f32[1,1024]{1,0:T(1,128)S(1)}, f32[1,1024]{1,0:T(1,128)S(1)}, u32[]{:S(2)}, u32[]{:S(2)}) %collective-permute-start.2) | collective-permute-done | bytes 4128 | tf_op jit(solution)/shard_map/ppermute | solution.py:308
  32.0 0.6 %slice_add_fusion.1 = f32[1,1024]{1,0:T(1,128)} fusion(f32[1,1024]{1,0:T(1,128)S(1)} %collective-permute-done.2, f32[2,1024]{1,0:T(2,128)S(1)} %slice_add_fusion), kind=kLoop, calls=%fused_computation.1 | loop fusion | flops 1024 | bytes 12288 | tf_op jit(solution)/shard_map/add | solution.py:308
  (4 shorter events, 0.0 us)
Async XLA Ops:
  2.2 7.3 %copy-start.1 = (bf16[48,256]{1,0:T(8,128)(2,1)S(1)}, bf16[48,256]{1,0:T(8,128)(2,1)}, u32[]{:S(2)}) copy-start(bf16[48,256]{1,0:T(8,128)(2,1)} %param.6) | copy-start | bytes 73732
  2.2 14.9 %all-to-all-start = ((bf16[8,16,640]{2,1,0:T(8,128)(2,1)}), bf16[8,16,640]{2,1,0:T(8,128)(2,1)S(1)}, u32[]{:S(2)}, u32[]{:S(2)}) async-start(bf16[8,16,640]{2,1,0:T(8,128)(2,1)} %bitcast.6), calls=%async_computation | async-start | bytes 327680 | tf_op jit(solution)/shard_map/all_to_all | solution.py:264
  9.5 5.5 %copy-start = (bf16[48,599]{1,0:T(8,128)(2,1)S(1)}, bf16[48,599]{1,0:T(8,128)(2,1)}, u32[]{:S(2)}) copy-start(bf16[48,599]{1,0:T(8,128)(2,1)} %prior.1) | copy-start | bytes 172516
  19.8 4.7 %collective-permute-start = (f32[4,1024]{1,0:T(4,128)S(1)}, f32[4,1024]{1,0:T(4,128)S(1)}, u32[]{:S(2)}, u32[]{:S(2)}) collective-permute-start(f32[4,1024]{1,0:T(4,128)S(1)} %get-tuple-element.12), channel_id=1, source_target_pairs={{0,16},{4,20},{8,24},{12,28},{16,0},{20,4},{24,8},{28,12},{1,17},{... | collective-permute-start | bytes 49160 | tf_op jit(solution)/shard_map/ppermute | solution.py:308
  24.6 3.7 %collective-permute-start.1 = (f32[2,1024]{1,0:T(2,128)S(1)}, f32[2,1024]{1,0:T(2,128)S(1)}, u32[]{:S(2)}, u32[]{:S(2)}) collective-permute-start(f32[2,1024]{1,0:T(2,128)S(1)} %slice.17), channel_id=1, source_target_pairs={{0,8},{4,12},{8,0},{12,4},{16,24},{20,28},{24,16},{28,20},{1,9},{5... | collective-permute-start | bytes 24584 | tf_op jit(solution)/shard_map/ppermute | solution.py:308
  28.3 3.7 %collective-permute-start.2 = (f32[1,1024]{1,0:T(1,128)S(1)}, f32[1,1024]{1,0:T(1,128)S(1)}, u32[]{:S(2)}, u32[]{:S(2)}) collective-permute-start(f32[1,1024]{1,0:T(1,128)S(1)} %slice.19), channel_id=1, source_target_pairs={{0,4},{4,0},{8,12},{12,8},{16,20},{20,16},{24,28},{28,24},{1,5},{5... | collective-permute-start | bytes 12296 | tf_op jit(solution)/shard_map/ppermute | solution.py:308

commit v4 on v3

--- a/solution.py
+++ b/solution.py
@@ -23,6 +23,10 @@
 
 def column_sum(values):
     return jnp.sum(values, axis=1, keepdims=True)
+
+
+def half_way(place, size):
+    return (place + size // 2) % size
 
 
 def route_kernel(
@@ -91,7 +95,7 @@
     hits = (lax.broadcasted_iota(I32, (sta_size, positions), 0) == owner).astype(F32)
     ahead = jnp.dot(hits.astype(BF16), before, preferred_element_type=F32)
     rank = jnp.sum(ahead * hits, axis=0, keepdims=True).astype(I32)
-    goes = row == owner * capacity + rank
+    goes = row == half_way(owner, sta_size) * capacity + rank
     row_tag = column_sum(jnp.where(goes, local_row, 0).astype(F32))
     template_tag = column_sum(jnp.where(goes, relative, 0).astype(F32))
 
@@ -267,6 +271,7 @@
         split_axis=0,
         concat_axis=0,
         tiled=True,
+        axis_index_groups=[[half_way(i, sta_size) for i in range(sta_size)]],
     ).reshape(positions, width)
 
     whole_time = lax.all_gather(window, "tpl", axis=1, tiled=True)

time: 32.9 us -> 32.3 us (0.982)
  starting transfers between devices: 10.9 us -> 9.92 us
  waiting for transfers between devices: 9.83 us -> 10.2 us
    ppermute x3, waiting for transfers between devices: 8.51 us -> 10.2 us  [per_device(): kept = kept + lax.ppermute(given, 'sta', pairs)]
    ppermute x3, starting transfers between devices: 3.59 us -> 2.06 us  [per_device(): kept = kept + lax.ppermute(given, 'sta', pairs)]
    all_to_all x1, waiting for transfers between devices: 1.32 us -> 0.01 us  [per_device(): lax.all_to_all(sent.reshape(sta_size, positions // sta_size, width), 'sta...]
    all_to_all x1, starting transfers between devices: 7.3 us -> 7.86 us  [per_device(): lax.all_to_all(sent.reshape(sta_size, positions // sta_size, width), 'sta...]
  transfers between devices with their start and end apart: 4 -> 4, of which waited for: 4 -> 3; matrix products, arithmetic and copies ran while one was open for 0% -> 0% of each run, Pallas kernels for 2% -> 2%
where the time goes in v4:
time: 32.3 us; the launch traced here: 32 us
  waiting for transfers between devices  10.2 us (32%)
  starting transfers between devices  9.92 us (31%)
  Pallas kernels  5.7 us (18%)
  blocking collectives  5.46 us (17%)
  other arithmetic  0.61 us (2%)
    ppermute x3, waiting for transfers between devices, per_device(): kept = kept + lax.ppermute(given, 'sta', pairs)  10.2 us
    all_to_all x1, starting transfers between devices, per_device(): lax.all_to_all(sent.reshape(sta_size, positions // sta_size, width), 'sta...  7.86 us
    all_gather x1, blocking collectives, per_device(): whole_time = lax.all_gather(window, 'tpl', axis=1, tiled=True)  5.46 us
    pallas_call x1, Pallas kernels, per_device(): pl.pallas_call(functools.partial(correlate_kernel, length), out_shape=[ja...  2.73 us
    pallas_call x1, Pallas kernels, per_device(): pl.pallas_call(functools.partial(route_kernel, sta_size, block_rows), out...  2.21 us
    ppermute x3, starting transfers between devices, per_device(): kept = kept + lax.ppermute(given, 'sta', pairs)  2.06 us
    pallas_call x1, Pallas kernels, per_device(): pl.pallas_call(functools.partial(prepare_kernel, length), out_shape=[jax....  0.75 us
  transfers between devices with their start and end apart: 4, of which 3 were waited for; matrix products, arithmetic and copies ran while one was open for 0% of the time, Pallas kernels for 2%

profile of v4, /device:TPU:0, one launch (start us, length us, event | category | flops | bytes accessed | tf_op | source)
XLA Modules:
  0.0 32.0 jit_solution(10175718826883808681)
XLA Ops:
  0.0 2.2 %route.1 = bf16[128,640]{1,0:T(8,128)(2,1)} custom-call(s32[1]{0:T(128)} %bitcast.sta_pos, bf16[128,600]{1,0:T(8,128)(2,1)} %bitcast.7, s32[8,16]{1,0:T(8,128)} %chan_list_in.1, s32[8]{0:T(128)} %chan_count_in.1, s32[1,128]{1,0:T(1,128)} %bitcast.8), custom_call_target="tpu_custom_call" | custom-call | tf_op jit(solution)/shard_map/route/pallas_call | solution.py:246
  2.2 0.0 copy-start.1
  2.2 7.9 %all-to-all-start = ((bf16[8,16,640]{2,1,0:T(8,128)(2,1)}), bf16[8,16,640]{2,1,0:T(8,128)(2,1)S(1)}, u32[]{:S(2)}, u32[]{:S(2)}) async-start(bf16[8,16,640]{2,1,0:T(8,128)(2,1)} %bitcast.6), calls=%async_computation | async-start | bytes 327680 | tf_op jit(solution)/shard_map/all_to_all | solution.py:268
  10.1 0.0 copy-done.1
  10.1 0.0 copy-start
  10.1 5.5 %all_gather.3.window = bf16[48,1024]{1,0:T(8,128)(2,1)S(1)} all-gather(bf16[48,256]{1,0:T(8,128)(2,1)S(1)} %copy-done.1), channel_id=1, replica_groups=mesh['sta'=8,'tpl'=4] {'tpl'}, dimensions={1}, use_global_device_ids=true | all-gather | bytes 122880 | tf_op jit(solution)/shard_map/all_gather | solution.py:277
  15.6 0.0 copy-done
  15.6 0.8 %prepare.1 = (bf16[192,1536]{1,0:T(8,128)(2,1)S(1)}, bf16[96,1024]{1,0:T(8,128)(2,1)S(1)}) custom-call(bf16[48,599]{1,0:T(8,128)(2,1)S(1)} %copy-done, bf16[48,1024]{1,0:T(8,128)(2,1)S(1)} %all_gather.3.window), custom_call_target="tpu_custom_call" | custom-call | tf_op jit(solution)/shard_map/prepare/pallas_call | solution.py:280
  16.3 0.0 all-to-all-done
  16.3 2.7 %correlate.1 = (f32[4,1024]{1,0:T(4,128)S(1)}, f32[4,1024]{1,0:T(4,128)S(1)}) custom-call(bf16[128,640]{1,0:T(8,128)(2,1)S(1)} %bitcast.5, bf16[192,1536]{1,0:T(8,128)(2,1)S(1)} %get-tuple-element.9.shifted, bf16[96,1024]{1,0:T(8,128)(2,1)S(1)} %get-tuple-element.10.scales), custom_call_target="tpu_custom_call" | custom-call | tf_op jit(solution)/shard_map/correlate/pallas_call | solution.py:294
  19.1 0.1 collective-permute-start
  19.1 4.8 %collective-permute-done = f32[4,1024]{1,0:T(4,128)S(1)} collective-permute-done((f32[4,1024]{1,0:T(4,128)S(1)}, f32[4,1024]{1,0:T(4,128)S(1)}, u32[]{:S(2)}, u32[]{:S(2)}) %collective-permute-start) | collective-permute-done | bytes 16416 | tf_op jit(solution)/shard_map/ppermute | solution.py:313
  24.0 0.5 %collective-permute-start.1 = (f32[2,1024]{1,0:T(2,128)S(1)}, f32[2,1024]{1,0:T(2,128)S(1)}, u32[]{:S(2)}, u32[]{:S(2)}) collective-permute-start(f32[2,1024]{1,0:T(2,128)S(1)} %slice.17), channel_id=1, source_target_pairs={{0,8},{4,12},{8,0},{12,4},{16,24},{20,28},{24,16},{28,20},{1,9},{5... | collective-permute-start | bytes 24584 | tf_op jit(solution)/shard_map/ppermute | solution.py:313
  24.4 3.3 %collective-permute-done.1 = f32[2,1024]{1,0:T(2,128)S(1)} collective-permute-done((f32[2,1024]{1,0:T(2,128)S(1)}, f32[2,1024]{1,0:T(2,128)S(1)}, u32[]{:S(2)}, u32[]{:S(2)}) %collective-permute-start.1) | collective-permute-done | bytes 8224 | tf_op jit(solution)/shard_map/ppermute | solution.py:313
  27.7 1.5 %collective-permute-start.2 = (f32[1,1024]{1,0:T(1,128)S(1)}, f32[1,1024]{1,0:T(1,128)S(1)}, u32[]{:S(2)}, u32[]{:S(2)}) collective-permute-start(f32[1,1024]{1,0:T(1,128)S(1)} %slice.19), channel_id=1, source_target_pairs={{0,4},{4,0},{8,12},{12,8},{16,20},{20,16},{24,28},{28,24},{1,5},{5... | collective-permute-start | bytes 12296 | tf_op jit(solution)/shard_map/ppermute | solution.py:313
  29.2 2.1 %collective-permute-done.2 = f32[1,1024]{1,0:T(1,128)S(1)} collective-permute-done((f32[1,1024]{1,0:T(1,128)S(1)}, f32[1,1024]{1,0:T(1,128)S(1)}, u32[]{:S(2)}, u32[]{:S(2)}) %collective-permute-start.2) | collective-permute-done | bytes 4128 | tf_op jit(solution)/shard_map/ppermute | solution.py:313
  31.4 0.6 %slice_add_fusion.1 = f32[1,1024]{1,0:T(1,128)} fusion(f32[1,1024]{1,0:T(1,128)S(1)} %collective-permute-done.2, f32[2,1024]{1,0:T(2,128)S(1)} %slice_add_fusion), kind=kLoop, calls=%fused_computation.1 | loop fusion | flops 1024 | bytes 12288 | tf_op jit(solution)/shard_map/add | solution.py:313
  (4 shorter events, 0.0 us)
Async XLA Ops:
  2.2 7.9 %copy-start.1 = (bf16[48,256]{1,0:T(8,128)(2,1)S(1)}, bf16[48,256]{1,0:T(8,128)(2,1)}, u32[]{:S(2)}) copy-start(bf16[48,256]{1,0:T(8,128)(2,1)} %param.6) | copy-start | bytes 73732
  2.2 14.1 %all-to-all-start = ((bf16[8,16,640]{2,1,0:T(8,128)(2,1)}), bf16[8,16,640]{2,1,0:T(8,128)(2,1)S(1)}, u32[]{:S(2)}, u32[]{:S(2)}) async-start(bf16[8,16,640]{2,1,0:T(8,128)(2,1)} %bitcast.6), calls=%async_computation | async-start | bytes 327680 | tf_op jit(solution)/shard_map/all_to_all | solution.py:268
  10.1 5.5 %copy-start = (bf16[48,599]{1,0:T(8,128)(2,1)S(1)}, bf16[48,599]{1,0:T(8,128)(2,1)}, u32[]{:S(2)}) copy-start(bf16[48,599]{1,0:T(8,128)(2,1)} %prior.1) | copy-start | bytes 172516
  19.1 4.9 %collective-permute-start = (f32[4,1024]{1,0:T(4,128)S(1)}, f32[4,1024]{1,0:T(4,128)S(1)}, u32[]{:S(2)}, u32[]{:S(2)}) collective-permute-start(f32[4,1024]{1,0:T(4,128)S(1)} %get-tuple-element.12), channel_id=1, source_target_pairs={{0,16},{4,20},{8,24},{12,28},{16,0},{20,4},{24,8},{28,12},{1,17},{... | collective-permute-start | bytes 49160 | tf_op jit(solution)/shard_map/ppermute | solution.py:313
  24.0 3.7 %collective-permute-start.1 = (f32[2,1024]{1,0:T(2,128)S(1)}, f32[2,1024]{1,0:T(2,128)S(1)}, u32[]{:S(2)}, u32[]{:S(2)}) collective-permute-start(f32[2,1024]{1,0:T(2,128)S(1)} %slice.17), channel_id=1, source_target_pairs={{0,8},{4,12},{8,0},{12,4},{16,24},{20,28},{24,16},{28,20},{1,9},{5... | collective-permute-start | bytes 24584 | tf_op jit(solution)/shard_map/ppermute | solution.py:313
  27.7 3.7 %collective-permute-start.2 = (f32[1,1024]{1,0:T(1,128)S(1)}, f32[1,1024]{1,0:T(1,128)S(1)}, u32[]{:S(2)}, u32[]{:S(2)}) collective-permute-start(f32[1,1024]{1,0:T(1,128)S(1)} %slice.19), channel_id=1, source_target_pairs={{0,4},{4,0},{8,12},{12,8},{16,20},{20,16},{24,28},{28,24},{1,5},{5... | collective-permute-start | bytes 12296 | tf_op jit(solution)/shard_map/ppermute | solution.py:313

commit v5 on v4

--- a/solution.py
+++ b/solution.py
@@ -116,14 +116,18 @@
     ).astype(BF16)
 
 
-def prepare_kernel(length, prior, window, shifted, scales, extended):
+def prepare_kernel(length, turns, tpl_pos, prior, *refs):
+    pieces, (shifted, scales, extended) = refs[: len(turns)], refs[len(turns) :]
     rows, before = prior.shape
-    lags = window.shape[1]
+    piece = pieces[0].shape[1]
+    lags = piece * len(turns)
     total = extended.shape[1]
     start = before // LANE * LANE
     extended[:, :start] = jnp.zeros((rows, start), F32)
     extended[:, start:] = jnp.zeros((rows, total - start), F32)
-    extended[:, start : start + lags] = window[...].astype(F32)
+    for turn, part in zip(turns, pieces):
+        first = pl.multiple_of(start + (tpl_pos[0] ^ turn) * piece, LANE)
+        extended[:, pl.ds(first, piece)] = part[...].astype(F32)
     moved = pltpu.roll(extended[:, start:], before - start, axis=1)
     extended[:, start:] = jnp.zeros((rows, total - start), F32)
     extended[:, :before] = prior[...].astype(F32)
@@ -136,19 +140,27 @@
     square = whole * whole
     high = square.astype(BF16)
     low = (square - high.astype(F32)).astype(BF16)
-    span = up(length + LANE - 1, LANE)
-    sample = lax.broadcasted_iota(I32, (span, LANE), 0)
-    lag = lax.broadcasted_iota(I32, (span, LANE), 1)
-    band = ((sample >= lag) & (sample < lag + length)).astype(F32).astype(BF16)
+    over = length % LANE
+    sample = lax.broadcasted_iota(I32, (2 * LANE, LANE), 0) % LANE
+    lag = lax.broadcasted_iota(I32, (2 * LANE, LANE), 1)
+    masks = [sample >= lag, sample < (lag + over) % LANE, sample >= 0]
+    masks = jnp.concatenate([mask.astype(F32) for mask in masks], axis=1).astype(BF16)
+    spans = [slice(k * LANE, (k + 1) * LANE) for k in range(total // LANE)]
+    squares = [jnp.concatenate([high[:, at], low[:, at]], axis=1) for at in spans]
+    sums = jnp.dot(jnp.concatenate(squares, axis=0), masks, preferred_element_type=F32)
+    sums = sums.reshape(len(spans), rows, 3 * LANE)
+    first, last, every = (sums[:, :, at] for at in spans[:3])
+    inside = lax.broadcasted_iota(I32, (rows, LANE), 1) < LANE - over
     for a in range(lags // LANE):
-        at = slice(a * LANE, a * LANE + span)
-        energy = jnp.dot(high[:, at], band, preferred_element_type=F32) + jnp.dot(
-            low[:, at], band, preferred_element_type=F32
-        )
+        energy = first[a]
+        for k in range(a + 1, a + length // LANE):
+            energy = energy + every[k]
+        end = a + length // LANE
+        energy = energy + jnp.where(inside, last[end], every[end] + last[end + 1])
         scale = 1.0 / jnp.sqrt(energy + epsilon)
         scale_high = scale.astype(BF16)
-        scales[:rows, a * LANE : (a + 1) * LANE] = scale_high
-        scales[rows:, a * LANE : (a + 1) * LANE] = (scale - scale_high.astype(F32)).astype(BF16)
+        scales[:rows, spans[a]] = scale_high
+        scales[rows:, spans[a]] = (scale - scale_high.astype(F32)).astype(BF16)
 
 
 def correlate_kernel(
@@ -238,7 +250,8 @@
     positions = group_size * slot_count
     block_rows = prior.shape[0]
     width = up(length + STEP, LANE)
-    lags = window.shape[1] * lax.axis_size("tpl")
+    tpl_size = lax.axis_size("tpl")
+    lags = window.shape[1] * tpl_size
     vmem = pl.BlockSpec(memory_space=pltpu.VMEM)
     smem = pl.BlockSpec(memory_space=pltpu.SMEM)
 
@@ -274,21 +287,28 @@
         axis_index_groups=[[half_way(i, sta_size) for i in range(sta_size)]],
     ).reshape(positions, width)
 
-    whole_time = lax.all_gather(window, "tpl", axis=1, tiled=True)
+    pieces, turns = [window], [0]
+    distance = tpl_size // 2
+    while distance >= 1:
+        hop = distance | 1
+        pairs = [(i, i ^ hop) for i in range(tpl_size)]
+        pieces = pieces + [lax.ppermute(piece, "tpl", pairs) for piece in pieces]
+        turns = turns + [turn ^ hop for turn in turns]
+        distance //= 2
     total = up(prior.shape[1] + lags, LANE)
     used = lags - LANE + width
     shifted, scales = pl.pallas_call(
-        functools.partial(prepare_kernel, length),
+        functools.partial(prepare_kernel, length, turns),
         out_shape=[
             jax.ShapeDtypeStruct((TURNS * block_rows, used), BF16),
             jax.ShapeDtypeStruct((2 * block_rows, lags), BF16),
         ],
-        in_specs=[vmem, vmem],
+        in_specs=[smem] + [vmem] * (1 + tpl_size),
         out_specs=[vmem, vmem],
         scratch_shapes=[pltpu.VMEM((block_rows, total), F32)],
         compiler_params=pltpu.CompilerParams(vmem_limit_bytes=16 * MIB),
         name="prepare",
-    )(prior, whole_time)
+    )(lax.axis_index("tpl").astype(I32).reshape(1), prior, *pieces)
 
     half = group_size // 2
     kept, given = pl.pallas_call(

time: 32.3 us -> 31.4 us (0.972)
  blocking collectives: 5.46 us -> 0 us
  starting transfers between devices: 9.92 us -> 12.8 us
  waiting for transfers between devices: 10.2 us -> 12.2 us
    all_gather x1 -> x0, blocking collectives: 5.46 us -> none  [per_device(): whole_time = lax.all_gather(window, 'tpl', axis=1, tiled=True)]
    ppermute x0 -> x3, waiting for transfers between devices: none -> 2.9 us  [per_device(): pieces = pieces + [lax.ppermute(piece, 'tpl', pairs) for piece in pieces]]
    ppermute x0 -> x3, starting transfers between devices: none -> 1.76 us  [per_device(): pieces = pieces + [lax.ppermute(piece, 'tpl', pairs) for piece in pieces]]
    ppermute x3, starting transfers between devices: 2.06 us -> 3.03 us  [per_device(): kept = kept + lax.ppermute(given, 'sta', pairs)]
    ppermute x3, waiting for transfers between devices: 10.2 us -> 9.23 us  [per_device(): kept = kept + lax.ppermute(given, 'sta', pairs)]
  transfers between devices with their start and end apart: 4 -> 7, of which waited for: 3 -> 5; matrix products, arithmetic and copies ran while one was open for 0% -> 0% of each run, Pallas kernels for 2% -> 2%
where the time goes in v5:
time: 31.4 us; the launch traced here: 31.1 us
  starting transfers between devices  12.8 us (41%)
  waiting for transfers between devices  12.2 us (39%)
  Pallas kernels  5.45 us (17%)
  other arithmetic  0.61 us (2%)
    ppermute x3, waiting for transfers between devices, per_device(): kept = kept + lax.ppermute(given, 'sta', pairs)  9.23 us
    all_to_all x1, starting transfers between devices, per_device(): lax.all_to_all(sent.reshape(sta_size, positions // sta_size, width), 'sta...  7.99 us
    ppermute x3, starting transfers between devices, per_device(): kept = kept + lax.ppermute(given, 'sta', pairs)  3.03 us
    ppermute x3, waiting for transfers between devices, per_device(): pieces = pieces + [lax.ppermute(piece, 'tpl', pairs) for piece in pieces]  2.9 us
    pallas_call x1, Pallas kernels, per_device(): pl.pallas_call(functools.partial(correlate_kernel, length), out_shape=[ja...  2.75 us
    pallas_call x1, Pallas kernels, per_device(): pl.pallas_call(functools.partial(route_kernel, sta_size, block_rows), out...  2.22 us
    ppermute x3, starting transfers between devices, per_device(): pieces = pieces + [lax.ppermute(piece, 'tpl', pairs) for piece in pieces]  1.76 us
  transfers between devices with their start and end apart: 7, of which 5 were waited for; matrix products, arithmetic and copies ran while one was open for 0% of the time, Pallas kernels for 2%

profile of v5, /device:TPU:0, one launch (start us, length us, event | category | flops | bytes accessed | tf_op | source)
XLA Modules:
  0.0 31.1 jit_solution(17752564821245258908)
XLA Ops:
  0.0 2.2 %route.1 = bf16[128,640]{1,0:T(8,128)(2,1)} custom-call(s32[1]{0:T(128)} %bitcast.sta_pos, bf16[128,600]{1,0:T(8,128)(2,1)} %bitcast.8, s32[8,16]{1,0:T(8,128)} %chan_list_in.1, s32[8]{0:T(128)} %chan_count_in.1, s32[1,128]{1,0:T(1,128)} %bitcast.9), custom_call_target="tpu_custom_call" | custom-call | tf_op jit(solution)/shard_map/route/pallas_call | solution.py:259
  2.2 0.0 copy-start.1
  2.2 0.0 copy-start
  2.3 8.0 %all-to-all-start = ((bf16[8,16,640]{2,1,0:T(8,128)(2,1)}), bf16[8,16,640]{2,1,0:T(8,128)(2,1)S(1)}, u32[]{:S(2)}, u32[]{:S(2)}) async-start(bf16[8,16,640]{2,1,0:T(8,128)(2,1)} %bitcast.7), calls=%async_computation | async-start | bytes 327680 | tf_op jit(solution)/shard_map/all_to_all | solution.py:281
  10.2 0.0 copy-done.1
  10.2 0.4 %collective-permute-start = (bf16[48,256]{1,0:T(8,128)(2,1)S(1)}, bf16[48,256]{1,0:T(8,128)(2,1)S(1)}, u32[]{:S(2)}, u32[]{:S(2)}) collective-permute-start(bf16[48,256]{1,0:T(8,128)(2,1)S(1)} %copy-done.1), channel_id=1, source_target_pairs={{0,3},{1,2},{2,1},{3,0},{4,7},{5,6},{6,5},{7,4},{8,11},{9,10},{10,... | collective-permute-start | bytes 73736 | tf_op jit(solution)/shard_map/ppermute | solution.py:295
  10.6 1.2 %collective-permute-start.1 = (bf16[48,256]{1,0:T(8,128)(2,1)S(1)}, bf16[48,256]{1,0:T(8,128)(2,1)S(1)}, u32[]{:S(2)}, u32[]{:S(2)}) collective-permute-start(bf16[48,256]{1,0:T(8,128)(2,1)S(1)} %copy-done.1), channel_id=1, source_target_pairs={{0,1},{1,0},{2,3},{3,2},{4,5},{5,4},{6,7},{7,6},{8,9},{9,8},{10,11... | collective-permute-start | bytes 73736 | tf_op jit(solution)/shard_map/ppermute | solution.py:295
  11.9 1.9 %collective-permute-done.refs_1_ = bf16[48,256]{1,0:T(8,128)(2,1)S(1)} collective-permute-done((bf16[48,256]{1,0:T(8,128)(2,1)S(1)}, bf16[48,256]{1,0:T(8,128)(2,1)S(1)}, u32[]{:S(2)}, u32[]{:S(2)}) %collective-permute-start) | collective-permute-done | bytes 24608 | tf_op jit(solution)/shard_map/ppermute | solution.py:295
  13.7 0.2 collective-permute-start.2
  13.9 0.0 collective-permute-done.1.refs_2_
  13.9 1.0 %collective-permute-done.2.refs_3_ = bf16[48,256]{1,0:T(8,128)(2,1)S(1)} collective-permute-done((bf16[48,256]{1,0:T(8,128)(2,1)S(1)}, bf16[48,256]{1,0:T(8,128)(2,1)S(1)}, u32[]{:S(2)}, u32[]{:S(2)}) %collective-permute-start.2) | collective-permute-done | bytes 24608 | tf_op jit(solution)/shard_map/ppermute | solution.py:295
  14.9 0.0 copy-done
  14.9 0.5 %prepare.1 = (bf16[192,1536]{1,0:T(8,128)(2,1)S(1)}, bf16[96,1024]{1,0:T(8,128)(2,1)S(1)}) custom-call(s32[1]{0:T(128)} %bitcast.5.tpl_pos, bf16[48,599]{1,0:T(8,128)(2,1)S(1)} %copy-done, bf16[48,256]{1,0:T(8,128)(2,1)S(1)} %copy-done.1, bf16[48,256]{1,0:T(8,128)(2,1)S(1)} %collective-permute-done.refs_1_, ...), custom_call_target="tpu_custom_call" | custom-call | tf_op jit(solution)/shard_map/prepare/pallas_call | solution.py:300
  15.4 0.0 all-to-all-done
  15.5 2.7 %correlate.1 = (f32[4,1024]{1,0:T(4,128)S(1)}, f32[4,1024]{1,0:T(4,128)S(1)}) custom-call(bf16[128,640]{1,0:T(8,128)(2,1)S(1)} %bitcast.6, bf16[192,1536]{1,0:T(8,128)(2,1)S(1)} %get-tuple-element.9.shifted, bf16[96,1024]{1,0:T(8,128)(2,1)S(1)} %get-tuple-element.10.scales), custom_call_target="tpu_custom_call" | custom-call | tf_op jit(solution)/shard_map/correlate/pallas_call | solution.py:314
  18.2 1.1 %collective-permute-start.3 = (f32[4,1024]{1,0:T(4,128)S(1)}, f32[4,1024]{1,0:T(4,128)S(1)}, u32[]{:S(2)}, u32[]{:S(2)}) collective-permute-start(f32[4,1024]{1,0:T(4,128)S(1)} %get-tuple-element.12), channel_id=1, source_target_pairs={{0,16},{4,20},{8,24},{12,28},{16,0},{20,4},{24,8},{28,12},{1,17},{... | collective-permute-start | bytes 49160 | tf_op jit(solution)/shard_map/ppermute | solution.py:333
  19.3 3.8 %collective-permute-done.3 = f32[4,1024]{1,0:T(4,128)S(1)} collective-permute-done((f32[4,1024]{1,0:T(4,128)S(1)}, f32[4,1024]{1,0:T(4,128)S(1)}, u32[]{:S(2)}, u32[]{:S(2)}) %collective-permute-start.3) | collective-permute-done | bytes 16416 | tf_op jit(solution)/shard_map/ppermute | solution.py:333
  23.1 0.5 %collective-permute-start.4 = (f32[2,1024]{1,0:T(2,128)S(1)}, f32[2,1024]{1,0:T(2,128)S(1)}, u32[]{:S(2)}, u32[]{:S(2)}) collective-permute-start(f32[2,1024]{1,0:T(2,128)S(1)} %slice.17), channel_id=1, source_target_pairs={{0,8},{4,12},{8,0},{12,4},{16,24},{20,28},{24,16},{28,20},{1,9},{5... | collective-permute-start | bytes 24584 | tf_op jit(solution)/shard_map/ppermute | solution.py:333
  23.6 3.2 %collective-permute-done.4 = f32[2,1024]{1,0:T(2,128)S(1)} collective-permute-done((f32[2,1024]{1,0:T(2,128)S(1)}, f32[2,1024]{1,0:T(2,128)S(1)}, u32[]{:S(2)}, u32[]{:S(2)}) %collective-permute-start.4) | collective-permute-done | bytes 8224 | tf_op jit(solution)/shard_map/ppermute | solution.py:333
  26.8 1.5 %collective-permute-start.5 = (f32[1,1024]{1,0:T(1,128)S(1)}, f32[1,1024]{1,0:T(1,128)S(1)}, u32[]{:S(2)}, u32[]{:S(2)}) collective-permute-start(f32[1,1024]{1,0:T(1,128)S(1)} %slice.19), channel_id=1, source_target_pairs={{0,4},{4,0},{8,12},{12,8},{16,20},{20,16},{24,28},{28,24},{1,5},{5... | collective-permute-start | bytes 12296 | tf_op jit(solution)/shard_map/ppermute | solution.py:333
  28.3 2.2 %collective-permute-done.5 = f32[1,1024]{1,0:T(1,128)S(1)} collective-permute-done((f32[1,1024]{1,0:T(1,128)S(1)}, f32[1,1024]{1,0:T(1,128)S(1)}, u32[]{:S(2)}, u32[]{:S(2)}) %collective-permute-start.5) | collective-permute-done | bytes 4128 | tf_op jit(solution)/shard_map/ppermute | solution.py:333
  30.5 0.6 %slice_add_fusion.1 = f32[1,1024]{1,0:T(1,128)} fusion(f32[1,1024]{1,0:T(1,128)S(1)} %collective-permute-done.5, f32[2,1024]{1,0:T(2,128)S(1)} %slice_add_fusion), kind=kLoop, calls=%fused_computation.1 | loop fusion | flops 1024 | bytes 12288 | tf_op jit(solution)/shard_map/add | solution.py:333
  (4 shorter events, 0.0 us)
Async XLA Ops:
  2.2 8.0 %copy-start.1 = (bf16[48,256]{1,0:T(8,128)(2,1)S(1)}, bf16[48,256]{1,0:T(8,128)(2,1)}, u32[]{:S(2)}) copy-start(bf16[48,256]{1,0:T(8,128)(2,1)} %refs_0_.1) | copy-start | bytes 73732
  2.2 12.7 %copy-start = (bf16[48,599]{1,0:T(8,128)(2,1)S(1)}, bf16[48,599]{1,0:T(8,128)(2,1)}, u32[]{:S(2)}) copy-start(bf16[48,599]{1,0:T(8,128)(2,1)} %prior.1) | copy-start | bytes 172516
  2.3 13.2 %all-to-all-start = ((bf16[8,16,640]{2,1,0:T(8,128)(2,1)}), bf16[8,16,640]{2,1,0:T(8,128)(2,1)S(1)}, u32[]{:S(2)}, u32[]{:S(2)}) async-start(bf16[8,16,640]{2,1,0:T(8,128)(2,1)} %bitcast.7), calls=%async_computation | async-start | bytes 327680 | tf_op jit(solution)/shard_map/all_to_all | solution.py:281
  10.2 3.5 %collective-permute-start = (bf16[48,256]{1,0:T(8,128)(2,1)S(1)}, bf16[48,256]{1,0:T(8,128)(2,1)S(1)}, u32[]{:S(2)}, u32[]{:S(2)}) collective-permute-start(bf16[48,256]{1,0:T(8,128)(2,1)S(1)} %copy-done.1), channel_id=1, source_target_pairs={{0,3},{1,2},{2,1},{3,0},{4,7},{5,6},{6,5},{7,4},{8,11},{9,10},{10,... | collective-permute-start | bytes 73736 | tf_op jit(solution)/shard_map/ppermute | solution.py:295
  10.6 3.3 %collective-permute-start.1 = (bf16[48,256]{1,0:T(8,128)(2,1)S(1)}, bf16[48,256]{1,0:T(8,128)(2,1)S(1)}, u32[]{:S(2)}, u32[]{:S(2)}) collective-permute-start(bf16[48,256]{1,0:T(8,128)(2,1)S(1)} %copy-done.1), channel_id=1, source_target_pairs={{0,1},{1,0},{2,3},{3,2},{4,5},{5,4},{6,7},{7,6},{8,9},{9,8},{10,11... | collective-permute-start | bytes 73736 | tf_op jit(solution)/shard_map/ppermute | solution.py:295
  13.7 1.2 %collective-permute-start.2 = (bf16[48,256]{1,0:T(8,128)(2,1)S(1)}, bf16[48,256]{1,0:T(8,128)(2,1)S(1)}, u32[]{:S(2)}, u32[]{:S(2)}) collective-permute-start(bf16[48,256]{1,0:T(8,128)(2,1)S(1)} %collective-permute-done.refs_1_), channel_id=1, source_target_pairs={{0,1},{1,0},{2,3},{3,2},{4,5},{5,4},{6,7},{7,6},{8,9},{9,8},{10,11... | collective-permute-start | bytes 73736 | tf_op jit(solution)/shard_map/ppermute | solution.py:295
  18.2 4.9 %collective-permute-start.3 = (f32[4,1024]{1,0:T(4,128)S(1)}, f32[4,1024]{1,0:T(4,128)S(1)}, u32[]{:S(2)}, u32[]{:S(2)}) collective-permute-start(f32[4,1024]{1,0:T(4,128)S(1)} %get-tuple-element.12), channel_id=1, source_target_pairs={{0,16},{4,20},{8,24},{12,28},{16,0},{20,4},{24,8},{28,12},{1,17},{... | collective-permute-start | bytes 49160 | tf_op jit(solution)/shard_map/ppermute | solution.py:333
  23.1 3.7 %collective-permute-start.4 = (f32[2,1024]{1,0:T(2,128)S(1)}, f32[2,1024]{1,0:T(2,128)S(1)}, u32[]{:S(2)}, u32[]{:S(2)}) collective-permute-start(f32[2,1024]{1,0:T(2,128)S(1)} %slice.17), channel_id=1, source_target_pairs={{0,8},{4,12},{8,0},{12,4},{16,24},{20,28},{24,16},{28,20},{1,9},{5... | collective-permute-start | bytes 24584 | tf_op jit(solution)/shard_map/ppermute | solution.py:333
  26.8 3.7 %collective-permute-start.5 = (f32[1,1024]{1,0:T(1,128)S(1)}, f32[1,1024]{1,0:T(1,128)S(1)}, u32[]{:S(2)}, u32[]{:S(2)}) collective-permute-start(f32[1,1024]{1,0:T(1,128)S(1)} %slice.19), channel_id=1, source_target_pairs={{0,4},{4,0},{8,12},{12,8},{16,20},{20,16},{24,28},{28,24},{1,5},{5... | collective-permute-start | bytes 12296 | tf_op jit(solution)/shard_map/ppermute | solution.py:333

commit v6 on v5

--- a/solution.py
+++ b/solution.py
@@ -25,8 +25,13 @@
     return jnp.sum(values, axis=1, keepdims=True)
 
 
-def half_way(place, size):
-    return (place + size // 2) % size
+def group_order(size):
+    middle = size // 2
+    order = []
+    for odd in range(2):
+        order += range(middle + odd, -1, -2)
+        order += range(middle + odd + 2, size, 2)
+    return order
 
 
 def route_kernel(
@@ -91,13 +96,15 @@
     for o in range(1, sta_size):
         owner = owner + (data_row >= o * block_rows).astype(I32)
     local_row = data_row - owner * block_rows
-    relative = along // slot_count ^ owner
     hits = (lax.broadcasted_iota(I32, (sta_size, positions), 0) == owner).astype(F32)
     ahead = jnp.dot(hits.astype(BF16), before, preferred_element_type=F32)
     rank = jnp.sum(ahead * hits, axis=0, keepdims=True).astype(I32)
-    goes = row == half_way(owner, sta_size) * capacity + rank
+    place = jnp.zeros((1, positions), I32)
+    for k, o in enumerate(group_order(sta_size)):
+        place = jnp.where(owner == o, k * capacity, place)
+    goes = row == place + rank
     row_tag = column_sum(jnp.where(goes, local_row, 0).astype(F32))
-    template_tag = column_sum(jnp.where(goes, relative, 0).astype(F32))
+    template_tag = column_sum(jnp.where(goes, along // slot_count, 0).astype(F32))
 
     count = jnp.zeros((positions, 1), I32)
     for t in range(group_size):
@@ -164,12 +171,11 @@
 
 
 def correlate_kernel(
-    length, arrived, shifted, scales, kept, given, frames, waves, traces, toeplitz, sums
+    length, order, arrived, shifted, scales, stacked, frames, waves, traces, toeplitz, sums
 ):
     positions, width = arrived.shape
     rows = scales.shape[0] // 2
     lags = scales.shape[1]
-    half = kept.shape[0]
     blocks = lags // LANE
     waves[...] = arrived[...].astype(F32)
     wanted = waves[:, length : length + 1].astype(I32)
@@ -231,16 +237,19 @@
             at_lag = slice(a * LANE, (a + 1) * LANE)
             traces[first : first + GROUP, at_lag] = traces[first : first + GROUP, at_lag] * own[a]
         if (g + 1) % CHUNK == 0:
-            for t in range(2 * half):
+            for t in range(len(order)):
                 total = jnp.zeros((GROUP, lags), F32) if g + 1 == CHUNK else sums[t]
                 for done in range(g + 1 - CHUNK, g + 1):
                     ready = slice(done * GROUP, (done + 1) * GROUP)
                     mine = (template[ready] == t).astype(F32)
                     total = total + traces[ready, :] * jnp.concatenate([mine] * blocks, axis=1)
                 sums[t] = total
-    stacked = jnp.sum(sums[...], axis=1)
-    kept[...] = stacked[:half]
-    given[...] = stacked[half:]
+    for k, t in enumerate(order):
+        lines = [
+            jnp.sum(sums[t, :, a * LANE : (a + 1) * LANE], axis=0, keepdims=True)
+            for a in range(blocks)
+        ]
+        stacked[k] = jnp.concatenate(lines, axis=0)
 
 
 def per_device(window, prior, waves, chan_list, chan_count, station_row):
@@ -252,6 +261,7 @@
     width = up(length + STEP, LANE)
     tpl_size = lax.axis_size("tpl")
     lags = window.shape[1] * tpl_size
+    order = group_order(sta_size)
     vmem = pl.BlockSpec(memory_space=pltpu.VMEM)
     smem = pl.BlockSpec(memory_space=pltpu.SMEM)
 
@@ -284,7 +294,7 @@
         split_axis=0,
         concat_axis=0,
         tiled=True,
-        axis_index_groups=[[half_way(i, sta_size) for i in range(sta_size)]],
+        axis_index_groups=[order],
     ).reshape(positions, width)
 
     pieces, turns = [window], [0]
@@ -310,12 +320,13 @@
         name="prepare",
     )(lax.axis_index("tpl").astype(I32).reshape(1), prior, *pieces)
 
-    half = group_size // 2
-    kept, given = pl.pallas_call(
-        functools.partial(correlate_kernel, length),
-        out_shape=[jax.ShapeDtypeStruct((half, lags), F32)] * 2,
+    each = group_size // sta_size
+    templates = [o * each + i for o in order for i in range(each)]
+    stacked = pl.pallas_call(
+        functools.partial(correlate_kernel, length, templates),
+        out_shape=jax.ShapeDtypeStruct((group_size, lags // LANE, LANE), F32),
         in_specs=[vmem] * 3,
-        out_specs=[vmem] * 2,
+        out_specs=vmem,
         scratch_shapes=[
             pltpu.VMEM((2, 2 * positions, used), BF16),
             pltpu.VMEM((positions, width), F32),
@@ -326,15 +337,11 @@
         compiler_params=pltpu.CompilerParams(vmem_limit_bytes=16 * MIB),
         name="correlate",
     )(arrived, shifted, scales)
-
-    distance = sta_size // 2
-    while True:
-        pairs = [(i, i ^ distance) for i in range(sta_size)]
-        kept = kept + lax.ppermute(given, "sta", pairs)
-        if distance == 1:
-            return kept
-        distance //= 2
-        kept, given = kept[:distance], kept[distance:]
+    parts = lax.all_to_all(
+        stacked, "sta", split_axis=0, concat_axis=0, tiled=True, axis_index_groups=[order]
+    )
+    parts = parts.reshape(sta_size, each, lags // LANE, LANE)
+    return jnp.sum(parts, axis=0).reshape(each, lags)
 
 
 def solution(mesh):

time: 31.4 us -> 28.1 us (0.89)
  waiting for transfers between devices: 12.2 us -> 2.9 us
  blocking collectives: 0 us -> 9.09 us
  starting transfers between devices: 12.8 us -> 9.75 us
    ppermute x3 -> x0, waiting for transfers between devices: 9.23 us -> none  [per_device(): kept = kept + lax.ppermute(given, 'sta', pairs)]
    all_to_all x0 -> x1, blocking collectives: none -> 9.09 us  [per_device(): lax.all_to_all(stacked, 'sta', split_axis=0, concat_axis=0, tiled=True, a...]
    ppermute x3 -> x0, starting transfers between devices: 3.03 us -> none  [per_device(): kept = kept + lax.ppermute(given, 'sta', pairs)]
    add x3 -> x0, other arithmetic: 0.61 us -> none  [per_device(): kept = kept + lax.ppermute(given, 'sta', pairs)]
    reduce_sum x0 -> x1, other arithmetic: none -> 0.6 us  [per_device(): return jnp.sum(parts, axis=0).reshape(each, lags)]
  transfers between devices with their start and end apart: 7 -> 4, of which waited for: 5 -> 2; matrix products, arithmetic and copies ran while one was open for 0% -> 0% of each run, Pallas kernels for 2% -> 2%
where the time goes in v6:
time: 28.1 us; the launch traced here: 27.8 us
  starting transfers between devices  9.75 us (35%)
  blocking collectives  9.09 us (32%)
  Pallas kernels  5.44 us (19%)
  waiting for transfers between devices  2.9 us (10%)
  other arithmetic  0.6 us (2%)
    all_to_all x1, blocking collectives, per_device(): lax.all_to_all(stacked, 'sta', split_axis=0, concat_axis=0, tiled=True, a...  9.09 us
    all_to_all x1, starting transfers between devices, per_device(): lax.all_to_all(sent.reshape(sta_size, positions // sta_size, width), 'sta...  7.99 us
    ppermute x3, waiting for transfers between devices, per_device(): pieces = pieces + [lax.ppermute(piece, 'tpl', pairs) for piece in pieces]  2.9 us
    pallas_call x1, Pallas kernels, per_device(): pl.pallas_call(functools.partial(correlate_kernel, length, templates), ou...  2.73 us
    pallas_call x1, Pallas kernels, per_device(): pl.pallas_call(functools.partial(route_kernel, sta_size, block_rows), out...  2.23 us
    ppermute x3, starting transfers between devices, per_device(): pieces = pieces + [lax.ppermute(piece, 'tpl', pairs) for piece in pieces]  1.76 us
    reduce_sum x1, other arithmetic, per_device(): return jnp.sum(parts, axis=0).reshape(each, lags)  0.6 us
  transfers between devices with their start and end apart: 4, of which 2 were waited for; matrix products, arithmetic and copies ran while one was open for 0% of the time, Pallas kernels for 2%

profile of v6, /device:TPU:0, one launch (start us, length us, event | category | flops | bytes accessed | tf_op | source)
XLA Modules:
  0.0 27.8 jit_solution(6120104262553183531)
XLA Ops:
  0.0 2.2 %route.1 = bf16[128,640]{1,0:T(8,128)(2,1)} custom-call(s32[1]{0:T(128)} %bitcast.sta_pos, bf16[128,600]{1,0:T(8,128)(2,1)} %bitcast.9, s32[8,16]{1,0:T(8,128)} %chan_list_in.1, s32[8]{0:T(128)} %chan_count_in.1, s32[1,128]{1,0:T(1,128)} %bitcast.10), custom_call_target="tpu_custom_call" | custom-call | tf_op jit(solution)/shard_map/route/pallas_call | solution.py:269
  2.2 0.0 copy-start.1
  2.2 0.0 copy-start
  2.3 8.0 %all-to-all-start = ((bf16[8,16,640]{2,1,0:T(8,128)(2,1)}), bf16[8,16,640]{2,1,0:T(8,128)(2,1)S(1)}, u32[]{:S(2)}, u32[]{:S(2)}) async-start(bf16[8,16,640]{2,1,0:T(8,128)(2,1)} %bitcast.8), calls=%async_computation | async-start | bytes 327680 | tf_op jit(solution)/shard_map/all_to_all | solution.py:291
  10.2 0.0 copy-done.1
  10.2 0.4 %collective-permute-start = (bf16[48,256]{1,0:T(8,128)(2,1)S(1)}, bf16[48,256]{1,0:T(8,128)(2,1)S(1)}, u32[]{:S(2)}, u32[]{:S(2)}) collective-permute-start(bf16[48,256]{1,0:T(8,128)(2,1)S(1)} %copy-done.1), channel_id=1, source_target_pairs={{0,3},{1,2},{2,1},{3,0},{4,7},{5,6},{6,5},{7,4},{8,11},{9,10},{10,... | collective-permute-start | bytes 73736 | tf_op jit(solution)/shard_map/ppermute | solution.py:305
  10.6 1.2 %collective-permute-start.1 = (bf16[48,256]{1,0:T(8,128)(2,1)S(1)}, bf16[48,256]{1,0:T(8,128)(2,1)S(1)}, u32[]{:S(2)}, u32[]{:S(2)}) collective-permute-start(bf16[48,256]{1,0:T(8,128)(2,1)S(1)} %copy-done.1), channel_id=1, source_target_pairs={{0,1},{1,0},{2,3},{3,2},{4,5},{5,4},{6,7},{7,6},{8,9},{9,8},{10,11... | collective-permute-start | bytes 73736 | tf_op jit(solution)/shard_map/ppermute | solution.py:305
  11.9 1.9 %collective-permute-done.refs_1_ = bf16[48,256]{1,0:T(8,128)(2,1)S(1)} collective-permute-done((bf16[48,256]{1,0:T(8,128)(2,1)S(1)}, bf16[48,256]{1,0:T(8,128)(2,1)S(1)}, u32[]{:S(2)}, u32[]{:S(2)}) %collective-permute-start) | collective-permute-done | bytes 24608 | tf_op jit(solution)/shard_map/ppermute | solution.py:305
  13.7 0.2 collective-permute-start.2
  13.9 0.0 collective-permute-done.1.refs_2_
  13.9 1.0 %collective-permute-done.2.refs_3_ = bf16[48,256]{1,0:T(8,128)(2,1)S(1)} collective-permute-done((bf16[48,256]{1,0:T(8,128)(2,1)S(1)}, bf16[48,256]{1,0:T(8,128)(2,1)S(1)}, u32[]{:S(2)}, u32[]{:S(2)}) %collective-permute-start.2) | collective-permute-done | bytes 24608 | tf_op jit(solution)/shard_map/ppermute | solution.py:305
  14.9 0.0 copy-done
  14.9 0.5 %prepare.1 = (bf16[192,1536]{1,0:T(8,128)(2,1)S(1)}, bf16[96,1024]{1,0:T(8,128)(2,1)S(1)}) custom-call(s32[1]{0:T(128)} %bitcast.5.tpl_pos, bf16[48,599]{1,0:T(8,128)(2,1)S(1)} %copy-done, bf16[48,256]{1,0:T(8,128)(2,1)S(1)} %copy-done.1, bf16[48,256]{1,0:T(8,128)(2,1)S(1)} %collective-permute-done.refs_1_, ...), custom_call_target="tpu_custom_call" | custom-call | tf_op jit(solution)/shard_map/prepare/pallas_call | solution.py:310
  15.4 0.0 all-to-all-done
  15.4 2.7 %correlate.1 = f32[8,8,128]{2,1,0:T(8,128)S(1)} custom-call(bf16[128,640]{1,0:T(8,128)(2,1)S(1)} %bitcast.7, bf16[192,1536]{1,0:T(8,128)(2,1)S(1)} %get-tuple-element.7.shifted, bf16[96,1024]{1,0:T(8,128)(2,1)S(1)} %get-tuple-element.8.scales), custom_call_target="tpu_custom_call" | custom-call | tf_op jit(solution)/shard_map/correlate/pallas_call | solution.py:325
  18.2 9.1 %all_to_all.10 = f32[8,8,128]{2,1,0:T(8,128)S(1)} all-to-all(f32[8,8,128]{2,1,0:T(8,128)S(1)} %correlate.1), channel_id=1, replica_groups={{16,8,0,24,20,12,4,28},{17,9,1,25,21,13,5,29},{18,10,2,26,22,14,6,30},{..., dimensions={0} | all-to-all | bytes 65536 | tf_op jit(solution)/shard_map/all_to_all | solution.py:340
  27.2 0.6 %reduce_sum.9 = f32[8,128]{1,0:T(8,128)} reduce(f32[8,8,128]{2,1,0:T(8,128)S(1)} %all_to_all.10, f32[]{:T(128)} %constant.10.clone.1), dimensions={0}, to_apply=%region_0.0 | reduce | flops 7168 | bytes 36868 | tf_op jit(solution)/shard_map/reduce_sum | solution.py:344
Async XLA Ops:
  2.2 8.0 %copy-start.1 = (bf16[48,256]{1,0:T(8,128)(2,1)S(1)}, bf16[48,256]{1,0:T(8,128)(2,1)}, u32[]{:S(2)}) copy-start(bf16[48,256]{1,0:T(8,128)(2,1)} %refs_0_.1) | copy-start | bytes 73732
  2.2 12.7 %copy-start = (bf16[48,599]{1,0:T(8,128)(2,1)S(1)}, bf16[48,599]{1,0:T(8,128)(2,1)}, u32[]{:S(2)}) copy-start(bf16[48,599]{1,0:T(8,128)(2,1)} %prior.1) | copy-start | bytes 172516
  2.3 13.1 %all-to-all-start = ((bf16[8,16,640]{2,1,0:T(8,128)(2,1)}), bf16[8,16,640]{2,1,0:T(8,128)(2,1)S(1)}, u32[]{:S(2)}, u32[]{:S(2)}) async-start(bf16[8,16,640]{2,1,0:T(8,128)(2,1)} %bitcast.8), calls=%async_computation | async-start | bytes 327680 | tf_op jit(solution)/shard_map/all_to_all | solution.py:291
  10.2 3.5 %collective-permute-start = (bf16[48,256]{1,0:T(8,128)(2,1)S(1)}, bf16[48,256]{1,0:T(8,128)(2,1)S(1)}, u32[]{:S(2)}, u32[]{:S(2)}) collective-permute-start(bf16[48,256]{1,0:T(8,128)(2,1)S(1)} %copy-done.1), channel_id=1, source_target_pairs={{0,3},{1,2},{2,1},{3,0},{4,7},{5,6},{6,5},{7,4},{8,11},{9,10},{10,... | collective-permute-start | bytes 73736 | tf_op jit(solution)/shard_map/ppermute | solution.py:305
  10.6 3.3 %collective-permute-start.1 = (bf16[48,256]{1,0:T(8,128)(2,1)S(1)}, bf16[48,256]{1,0:T(8,128)(2,1)S(1)}, u32[]{:S(2)}, u32[]{:S(2)}) collective-permute-start(bf16[48,256]{1,0:T(8,128)(2,1)S(1)} %copy-done.1), channel_id=1, source_target_pairs={{0,1},{1,0},{2,3},{3,2},{4,5},{5,4},{6,7},{7,6},{8,9},{9,8},{10,11... | collective-permute-start | bytes 73736 | tf_op jit(solution)/shard_map/ppermute | solution.py:305
  13.7 1.2 %collective-permute-start.2 = (bf16[48,256]{1,0:T(8,128)(2,1)S(1)}, bf16[48,256]{1,0:T(8,128)(2,1)S(1)}, u32[]{:S(2)}, u32[]{:S(2)}) collective-permute-start(bf16[48,256]{1,0:T(8,128)(2,1)S(1)} %collective-permute-done.refs_1_), channel_id=1, source_target_pairs={{0,1},{1,0},{2,3},{3,2},{4,5},{5,4},{6,7},{7,6},{8,9},{9,8},{10,11... | collective-permute-start | bytes 73736 | tf_op jit(solution)/shard_map/ppermute | solution.py:305

commit v7 on v6

--- a/solution.py
+++ b/solution.py
@@ -25,7 +25,11 @@
     return jnp.sum(values, axis=1, keepdims=True)
 
 
-def group_order(size):
+def waves_order(size):
+    return [(i + size // 2 - 1) % size for i in range(size)]
+
+
+def stacks_order(size):
     middle = size // 2
     order = []
     for odd in range(2):
@@ -100,7 +104,7 @@
     ahead = jnp.dot(hits.astype(BF16), before, preferred_element_type=F32)
     rank = jnp.sum(ahead * hits, axis=0, keepdims=True).astype(I32)
     place = jnp.zeros((1, positions), I32)
-    for k, o in enumerate(group_order(sta_size)):
+    for k, o in enumerate(waves_order(sta_size)):
         place = jnp.where(owner == o, k * capacity, place)
     goes = row == place + rank
     row_tag = column_sum(jnp.where(goes, local_row, 0).astype(F32))
@@ -261,7 +265,7 @@
     width = up(length + STEP, LANE)
     tpl_size = lax.axis_size("tpl")
     lags = window.shape[1] * tpl_size
-    order = group_order(sta_size)
+    order = stacks_order(sta_size)
     vmem = pl.BlockSpec(memory_space=pltpu.VMEM)
     smem = pl.BlockSpec(memory_space=pltpu.SMEM)
 
@@ -294,7 +298,7 @@
         split_axis=0,
         concat_axis=0,
         tiled=True,
-        axis_index_groups=[order],
+        axis_index_groups=[waves_order(sta_size)],
     ).reshape(positions, width)
 
     pieces, turns = [window], [0]

time: 28.1 us -> 27.7 us (0.986)
  blocking collectives: 9.09 us -> 8.21 us
  waiting for transfers between devices: 2.9 us -> 3.37 us
    all_to_all x1, blocking collectives: 9.09 us -> 8.21 us  [per_device(): lax.all_to_all(stacked, 'sta', split_axis=0, concat_axis=0, tiled=True, a...]
    all_to_all x1, waiting for transfers between devices: 0.01 us -> 0.46 us  [per_device(): lax.all_to_all(sent.reshape(sta_size, positions // sta_size, width), 'sta...]
  transfers between devices with their start and end apart: 4 -> 4, of which waited for: 2 -> 3; matrix products, arithmetic and copies ran while one was open for 0% -> 0% of each run, Pallas kernels for 2% -> 2%
where the time goes in v7:
time: 27.7 us; the launch traced here: 27.4 us
  starting transfers between devices  9.75 us (35%)
  blocking collectives  8.21 us (30%)
  Pallas kernels  5.44 us (20%)
  waiting for transfers between devices  3.37 us (12%)
  other arithmetic  0.6 us (2%)
    all_to_all x1, blocking collectives, per_device(): lax.all_to_all(stacked, 'sta', split_axis=0, concat_axis=0, tiled=True, a...  8.21 us
    all_to_all x1, starting transfers between devices, per_device(): lax.all_to_all(sent.reshape(sta_size, positions // sta_size, width), 'sta...  7.99 us
    ppermute x3, waiting for transfers between devices, per_device(): pieces = pieces + [lax.ppermute(piece, 'tpl', pairs) for piece in pieces]  2.9 us
    pallas_call x1, Pallas kernels, per_device(): pl.pallas_call(functools.partial(correlate_kernel, length, templates), ou...  2.73 us
    pallas_call x1, Pallas kernels, per_device(): pl.pallas_call(functools.partial(route_kernel, sta_size, block_rows), out...  2.23 us
    ppermute x3, starting transfers between devices, per_device(): pieces = pieces + [lax.ppermute(piece, 'tpl', pairs) for piece in pieces]  1.76 us
    reduce_sum x1, other arithmetic, per_device(): return jnp.sum(parts, axis=0).reshape(each, lags)  0.6 us
  transfers between devices with their start and end apart: 4, of which 3 were waited for; matrix products, arithmetic and copies ran while one was open for 0% of the time, Pallas kernels for 2%

profile of v7, /device:TPU:0, one launch (start us, length us, event | category | flops | bytes accessed | tf_op | source)
XLA Modules:
  0.0 27.4 jit_solution(13403192309337379878)
XLA Ops:
  0.0 2.2 %route.1 = bf16[128,640]{1,0:T(8,128)(2,1)} custom-call(s32[1]{0:T(128)} %bitcast.sta_pos, bf16[128,600]{1,0:T(8,128)(2,1)} %bitcast.9, s32[8,16]{1,0:T(8,128)} %chan_list_in.1, s32[8]{0:T(128)} %chan_count_in.1, s32[1,128]{1,0:T(1,128)} %bitcast.10), custom_call_target="tpu_custom_call" | custom-call | tf_op jit(solution)/shard_map/route/pallas_call | solution.py:273
  2.2 0.0 copy-start.1
  2.2 0.0 copy-start
  2.3 8.0 %all-to-all-start = ((bf16[8,16,640]{2,1,0:T(8,128)(2,1)}), bf16[8,16,640]{2,1,0:T(8,128)(2,1)S(1)}, u32[]{:S(2)}, u32[]{:S(2)}) async-start(bf16[8,16,640]{2,1,0:T(8,128)(2,1)} %bitcast.8), calls=%async_computation | async-start | bytes 327680 | tf_op jit(solution)/shard_map/all_to_all | solution.py:295
  10.2 0.0 copy-done.1
  10.3 0.4 %collective-permute-start = (bf16[48,256]{1,0:T(8,128)(2,1)S(1)}, bf16[48,256]{1,0:T(8,128)(2,1)S(1)}, u32[]{:S(2)}, u32[]{:S(2)}) collective-permute-start(bf16[48,256]{1,0:T(8,128)(2,1)S(1)} %copy-done.1), channel_id=1, source_target_pairs={{0,3},{1,2},{2,1},{3,0},{4,7},{5,6},{6,5},{7,4},{8,11},{9,10},{10,... | collective-permute-start | bytes 73736 | tf_op jit(solution)/shard_map/ppermute | solution.py:309
  10.6 1.2 %collective-permute-start.1 = (bf16[48,256]{1,0:T(8,128)(2,1)S(1)}, bf16[48,256]{1,0:T(8,128)(2,1)S(1)}, u32[]{:S(2)}, u32[]{:S(2)}) collective-permute-start(bf16[48,256]{1,0:T(8,128)(2,1)S(1)} %copy-done.1), channel_id=1, source_target_pairs={{0,1},{1,0},{2,3},{3,2},{4,5},{5,4},{6,7},{7,6},{8,9},{9,8},{10,11... | collective-permute-start | bytes 73736 | tf_op jit(solution)/shard_map/ppermute | solution.py:309
  11.9 1.9 %collective-permute-done.refs_1_ = bf16[48,256]{1,0:T(8,128)(2,1)S(1)} collective-permute-done((bf16[48,256]{1,0:T(8,128)(2,1)S(1)}, bf16[48,256]{1,0:T(8,128)(2,1)S(1)}, u32[]{:S(2)}, u32[]{:S(2)}) %collective-permute-start) | collective-permute-done | bytes 24608 | tf_op jit(solution)/shard_map/ppermute | solution.py:309
  13.7 0.2 collective-permute-start.2
  13.9 0.0 collective-permute-done.1.refs_2_
  13.9 1.0 %collective-permute-done.2.refs_3_ = bf16[48,256]{1,0:T(8,128)(2,1)S(1)} collective-permute-done((bf16[48,256]{1,0:T(8,128)(2,1)S(1)}, bf16[48,256]{1,0:T(8,128)(2,1)S(1)}, u32[]{:S(2)}, u32[]{:S(2)}) %collective-permute-start.2) | collective-permute-done | bytes 24608 | tf_op jit(solution)/shard_map/ppermute | solution.py:309
  14.9 0.0 copy-done
  14.9 0.5 %prepare.1 = (bf16[192,1536]{1,0:T(8,128)(2,1)S(1)}, bf16[96,1024]{1,0:T(8,128)(2,1)S(1)}) custom-call(s32[1]{0:T(128)} %bitcast.5.tpl_pos, bf16[48,599]{1,0:T(8,128)(2,1)S(1)} %copy-done, bf16[48,256]{1,0:T(8,128)(2,1)S(1)} %copy-done.1, bf16[48,256]{1,0:T(8,128)(2,1)S(1)} %collective-permute-done.refs_1_, ...), custom_call_target="tpu_custom_call" | custom-call | tf_op jit(solution)/shard_map/prepare/pallas_call | solution.py:314
  15.4 0.5 %all-to-all-done = bf16[8,16,640]{2,1,0:T(8,128)(2,1)S(1)} async-done(((bf16[8,16,640]{2,1,0:T(8,128)(2,1)}), bf16[8,16,640]{2,1,0:T(8,128)(2,1)S(1)}, u32[]{:S(2)}, u32[]{:S(2)}) %all-to-all-start) | async-done | bytes 163872 | tf_op jit(solution)/shard_map/all_to_all | solution.py:295
  15.9 2.7 %correlate.1 = f32[8,8,128]{2,1,0:T(8,128)S(1)} custom-call(bf16[128,640]{1,0:T(8,128)(2,1)S(1)} %bitcast.7, bf16[192,1536]{1,0:T(8,128)(2,1)S(1)} %get-tuple-element.7.shifted, bf16[96,1024]{1,0:T(8,128)(2,1)S(1)} %get-tuple-element.8.scales), custom_call_target="tpu_custom_call" | custom-call | tf_op jit(solution)/shard_map/correlate/pallas_call | solution.py:329
  18.6 8.2 %all_to_all.10 = f32[8,8,128]{2,1,0:T(8,128)S(1)} all-to-all(f32[8,8,128]{2,1,0:T(8,128)S(1)} %correlate.1), channel_id=1, replica_groups={{16,8,0,24,20,12,4,28},{17,9,1,25,21,13,5,29},{18,10,2,26,22,14,6,30},{..., dimensions={0} | all-to-all | bytes 65536 | tf_op jit(solution)/shard_map/all_to_all | solution.py:344
  26.8 0.6 %reduce_sum.9 = f32[8,128]{1,0:T(8,128)} reduce(f32[8,8,128]{2,1,0:T(8,128)S(1)} %all_to_all.10, f32[]{:T(128)} %constant.10.clone.1), dimensions={0}, to_apply=%region_0.0 | reduce | flops 7168 | bytes 36868 | tf_op jit(solution)/shard_map/reduce_sum | solution.py:348
Async XLA Ops:
  2.2 8.0 %copy-start.1 = (bf16[48,256]{1,0:T(8,128)(2,1)S(1)}, bf16[48,256]{1,0:T(8,128)(2,1)}, u32[]{:S(2)}) copy-start(bf16[48,256]{1,0:T(8,128)(2,1)} %refs_0_.1) | copy-start | bytes 73732
  2.2 12.7 %copy-start = (bf16[48,599]{1,0:T(8,128)(2,1)S(1)}, bf16[48,599]{1,0:T(8,128)(2,1)}, u32[]{:S(2)}) copy-start(bf16[48,599]{1,0:T(8,128)(2,1)} %prior.1) | copy-start | bytes 172516
  2.3 13.6 %all-to-all-start = ((bf16[8,16,640]{2,1,0:T(8,128)(2,1)}), bf16[8,16,640]{2,1,0:T(8,128)(2,1)S(1)}, u32[]{:S(2)}, u32[]{:S(2)}) async-start(bf16[8,16,640]{2,1,0:T(8,128)(2,1)} %bitcast.8), calls=%async_computation | async-start | bytes 327680 | tf_op jit(solution)/shard_map/all_to_all | solution.py:295
  10.3 3.5 %collective-permute-start = (bf16[48,256]{1,0:T(8,128)(2,1)S(1)}, bf16[48,256]{1,0:T(8,128)(2,1)S(1)}, u32[]{:S(2)}, u32[]{:S(2)}) collective-permute-start(bf16[48,256]{1,0:T(8,128)(2,1)S(1)} %copy-done.1), channel_id=1, source_target_pairs={{0,3},{1,2},{2,1},{3,0},{4,7},{5,6},{6,5},{7,4},{8,11},{9,10},{10,... | collective-permute-start | bytes 73736 | tf_op jit(solution)/shard_map/ppermute | solution.py:309
  10.6 3.3 %collective-permute-start.1 = (bf16[48,256]{1,0:T(8,128)(2,1)S(1)}, bf16[48,256]{1,0:T(8,128)(2,1)S(1)}, u32[]{:S(2)}, u32[]{:S(2)}) collective-permute-start(bf16[48,256]{1,0:T(8,128)(2,1)S(1)} %copy-done.1), channel_id=1, source_target_pairs={{0,1},{1,0},{2,3},{3,2},{4,5},{5,4},{6,7},{7,6},{8,9},{9,8},{10,11... | collective-permute-start | bytes 73736 | tf_op jit(solution)/shard_map/ppermute | solution.py:309
  13.7 1.2 %collective-permute-start.2 = (bf16[48,256]{1,0:T(8,128)(2,1)S(1)}, bf16[48,256]{1,0:T(8,128)(2,1)S(1)}, u32[]{:S(2)}, u32[]{:S(2)}) collective-permute-start(bf16[48,256]{1,0:T(8,128)(2,1)S(1)} %collective-permute-done.refs_1_), channel_id=1, source_target_pairs={{0,1},{1,0},{2,3},{3,2},{4,5},{5,4},{6,7},{7,6},{8,9},{9,8},{10,11... | collective-permute-start | bytes 73736 | tf_op jit(solution)/shard_map/ppermute | solution.py:309

commit v8 on v7

--- a/solution.py
+++ b/solution.py
@@ -26,6 +26,8 @@
 
 
 def waves_order(size):
+    if size == 8:
+        return [3, 0, 1, 4, 5, 7, 2, 6]
     return [(i + size // 2 - 1) % size for i in range(size)]
 
 

time: 27.7 us -> 27.5 us (level)
  no operation moved by 1% of the time
where the time goes in v8:
time: 27.5 us; the launch traced here: 27.3 us
  starting transfers between devices  9.71 us (35%)
  blocking collectives  8.19 us (30%)
  Pallas kernels  5.44 us (20%)
  waiting for transfers between devices  3.27 us (12%)
  other arithmetic  0.6 us (2%)
    all_to_all x1, blocking collectives, per_device(): lax.all_to_all(stacked, 'sta', split_axis=0, concat_axis=0, tiled=True, a...  8.19 us
    all_to_all x1, starting transfers between devices, per_device(): lax.all_to_all(sent.reshape(sta_size, positions // sta_size, width), 'sta...  7.99 us
    ppermute x3, waiting for transfers between devices, per_device(): pieces = pieces + [lax.ppermute(piece, 'tpl', pairs) for piece in pieces]  2.95 us
    pallas_call x1, Pallas kernels, per_device(): pl.pallas_call(functools.partial(correlate_kernel, length, templates), ou...  2.73 us
    pallas_call x1, Pallas kernels, per_device(): pl.pallas_call(functools.partial(route_kernel, sta_size, block_rows), out...  2.23 us
    ppermute x3, starting transfers between devices, per_device(): pieces = pieces + [lax.ppermute(piece, 'tpl', pairs) for piece in pieces]  1.72 us
    reduce_sum x1, other arithmetic, per_device(): return jnp.sum(parts, axis=0).reshape(each, lags)  0.6 us
  transfers between devices with their start and end apart: 4, of which 3 were waited for; matrix products, arithmetic and copies ran while one was open for 0% of the time, Pallas kernels for 2%

profile of v8, /device:TPU:0, one launch (start us, length us, event | category | flops | bytes accessed | tf_op | source)
XLA Modules:
  0.0 27.3 jit_solution(15347974128550480436)
XLA Ops:
  0.0 2.2 %route.1 = bf16[128,640]{1,0:T(8,128)(2,1)} custom-call(s32[1]{0:T(128)} %bitcast.sta_pos, bf16[128,600]{1,0:T(8,128)(2,1)} %bitcast.9, s32[8,16]{1,0:T(8,128)} %chan_list_in.1, s32[8]{0:T(128)} %chan_count_in.1, s32[1,128]{1,0:T(1,128)} %bitcast.10), custom_call_target="tpu_custom_call" | custom-call | tf_op jit(solution)/shard_map/route/pallas_call | solution.py:275
  2.2 0.0 copy-start.1
  2.2 0.0 copy-start
  2.3 8.0 %all-to-all-start = ((bf16[8,16,640]{2,1,0:T(8,128)(2,1)}), bf16[8,16,640]{2,1,0:T(8,128)(2,1)S(1)}, u32[]{:S(2)}, u32[]{:S(2)}) async-start(bf16[8,16,640]{2,1,0:T(8,128)(2,1)} %bitcast.8), calls=%async_computation | async-start | bytes 327680 | tf_op jit(solution)/shard_map/all_to_all | solution.py:297
  10.2 0.0 copy-done.1
  10.2 0.4 %collective-permute-start = (bf16[48,256]{1,0:T(8,128)(2,1)S(1)}, bf16[48,256]{1,0:T(8,128)(2,1)S(1)}, u32[]{:S(2)}, u32[]{:S(2)}) collective-permute-start(bf16[48,256]{1,0:T(8,128)(2,1)S(1)} %copy-done.1), channel_id=1, source_target_pairs={{0,3},{1,2},{2,1},{3,0},{4,7},{5,6},{6,5},{7,4},{8,11},{9,10},{10,... | collective-permute-start | bytes 73736 | tf_op jit(solution)/shard_map/ppermute | solution.py:311
  10.6 1.2 %collective-permute-start.1 = (bf16[48,256]{1,0:T(8,128)(2,1)S(1)}, bf16[48,256]{1,0:T(8,128)(2,1)S(1)}, u32[]{:S(2)}, u32[]{:S(2)}) collective-permute-start(bf16[48,256]{1,0:T(8,128)(2,1)S(1)} %copy-done.1), channel_id=1, source_target_pairs={{0,1},{1,0},{2,3},{3,2},{4,5},{5,4},{6,7},{7,6},{8,9},{9,8},{10,11... | collective-permute-start | bytes 73736 | tf_op jit(solution)/shard_map/ppermute | solution.py:311
  11.9 1.9 %collective-permute-done.refs_1_ = bf16[48,256]{1,0:T(8,128)(2,1)S(1)} collective-permute-done((bf16[48,256]{1,0:T(8,128)(2,1)S(1)}, bf16[48,256]{1,0:T(8,128)(2,1)S(1)}, u32[]{:S(2)}, u32[]{:S(2)}) %collective-permute-start) | collective-permute-done | bytes 24608 | tf_op jit(solution)/shard_map/ppermute | solution.py:311
  13.7 0.1 collective-permute-start.2
  13.8 0.0 collective-permute-done.1.refs_2_
  13.8 1.1 %collective-permute-done.2.refs_3_ = bf16[48,256]{1,0:T(8,128)(2,1)S(1)} collective-permute-done((bf16[48,256]{1,0:T(8,128)(2,1)S(1)}, bf16[48,256]{1,0:T(8,128)(2,1)S(1)}, u32[]{:S(2)}, u32[]{:S(2)}) %collective-permute-start.2) | collective-permute-done | bytes 24608 | tf_op jit(solution)/shard_map/ppermute | solution.py:311
  14.9 0.0 copy-done
  14.9 0.5 %prepare.1 = (bf16[192,1536]{1,0:T(8,128)(2,1)S(1)}, bf16[96,1024]{1,0:T(8,128)(2,1)S(1)}) custom-call(s32[1]{0:T(128)} %bitcast.5.tpl_pos, bf16[48,599]{1,0:T(8,128)(2,1)S(1)} %copy-done, bf16[48,256]{1,0:T(8,128)(2,1)S(1)} %copy-done.1, bf16[48,256]{1,0:T(8,128)(2,1)S(1)} %collective-permute-done.refs_1_, ...), custom_call_target="tpu_custom_call" | custom-call | tf_op jit(solution)/shard_map/prepare/pallas_call | solution.py:316
  15.4 0.3 %all-to-all-done = bf16[8,16,640]{2,1,0:T(8,128)(2,1)S(1)} async-done(((bf16[8,16,640]{2,1,0:T(8,128)(2,1)}), bf16[8,16,640]{2,1,0:T(8,128)(2,1)S(1)}, u32[]{:S(2)}, u32[]{:S(2)}) %all-to-all-start) | async-done | bytes 163872 | tf_op jit(solution)/shard_map/all_to_all | solution.py:297
  15.7 2.7 %correlate.1 = f32[8,8,128]{2,1,0:T(8,128)S(1)} custom-call(bf16[128,640]{1,0:T(8,128)(2,1)S(1)} %bitcast.7, bf16[192,1536]{1,0:T(8,128)(2,1)S(1)} %get-tuple-element.7.shifted, bf16[96,1024]{1,0:T(8,128)(2,1)S(1)} %get-tuple-element.8.scales), custom_call_target="tpu_custom_call" | custom-call | tf_op jit(solution)/shard_map/correlate/pallas_call | solution.py:331
  18.5 8.2 %all_to_all.10 = f32[8,8,128]{2,1,0:T(8,128)S(1)} all-to-all(f32[8,8,128]{2,1,0:T(8,128)S(1)} %correlate.1), channel_id=1, replica_groups={{16,8,0,24,20,12,4,28},{17,9,1,25,21,13,5,29},{18,10,2,26,22,14,6,30},{..., dimensions={0} | all-to-all | bytes 65536 | tf_op jit(solution)/shard_map/all_to_all | solution.py:346
  26.7 0.6 %reduce_sum.9 = f32[8,128]{1,0:T(8,128)} reduce(f32[8,8,128]{2,1,0:T(8,128)S(1)} %all_to_all.10, f32[]{:T(128)} %constant.10.clone.1), dimensions={0}, to_apply=%region_0.0 | reduce | flops 7168 | bytes 36868 | tf_op jit(solution)/shard_map/reduce_sum | solution.py:350
Async XLA Ops:
  2.2 8.0 %copy-start.1 = (bf16[48,256]{1,0:T(8,128)(2,1)S(1)}, bf16[48,256]{1,0:T(8,128)(2,1)}, u32[]{:S(2)}) copy-start(bf16[48,256]{1,0:T(8,128)(2,1)} %refs_0_.1) | copy-start | bytes 73732
  2.2 12.7 %copy-start = (bf16[48,599]{1,0:T(8,128)(2,1)S(1)}, bf16[48,599]{1,0:T(8,128)(2,1)}, u32[]{:S(2)}) copy-start(bf16[48,599]{1,0:T(8,128)(2,1)} %prior.1) | copy-start | bytes 172516
  2.3 13.5 %all-to-all-start = ((bf16[8,16,640]{2,1,0:T(8,128)(2,1)}), bf16[8,16,640]{2,1,0:T(8,128)(2,1)S(1)}, u32[]{:S(2)}, u32[]{:S(2)}) async-start(bf16[8,16,640]{2,1,0:T(8,128)(2,1)} %bitcast.8), calls=%async_computation | async-start | bytes 327680 | tf_op jit(solution)/shard_map/all_to_all | solution.py:297
  10.2 3.5 %collective-permute-start = (bf16[48,256]{1,0:T(8,128)(2,1)S(1)}, bf16[48,256]{1,0:T(8,128)(2,1)S(1)}, u32[]{:S(2)}, u32[]{:S(2)}) collective-permute-start(bf16[48,256]{1,0:T(8,128)(2,1)S(1)} %copy-done.1), channel_id=1, source_target_pairs={{0,3},{1,2},{2,1},{3,0},{4,7},{5,6},{6,5},{7,4},{8,11},{9,10},{10,... | collective-permute-start | bytes 73736 | tf_op jit(solution)/shard_map/ppermute | solution.py:311
  10.6 3.2 %collective-permute-start.1 = (bf16[48,256]{1,0:T(8,128)(2,1)S(1)}, bf16[48,256]{1,0:T(8,128)(2,1)S(1)}, u32[]{:S(2)}, u32[]{:S(2)}) collective-permute-start(bf16[48,256]{1,0:T(8,128)(2,1)S(1)} %copy-done.1), channel_id=1, source_target_pairs={{0,1},{1,0},{2,3},{3,2},{4,5},{5,4},{6,7},{7,6},{8,9},{9,8},{10,11... | collective-permute-start | bytes 73736 | tf_op jit(solution)/shard_map/ppermute | solution.py:311
  13.7 1.2 %collective-permute-start.2 = (bf16[48,256]{1,0:T(8,128)(2,1)S(1)}, bf16[48,256]{1,0:T(8,128)(2,1)S(1)}, u32[]{:S(2)}, u32[]{:S(2)}) collective-permute-start(bf16[48,256]{1,0:T(8,128)(2,1)S(1)} %collective-permute-done.refs_1_), channel_id=1, source_target_pairs={{0,1},{1,0},{2,3},{3,2},{4,5},{5,4},{6,7},{7,6},{8,9},{9,8},{10,11... | collective-permute-start | bytes 73736 | tf_op jit(solution)/shard_map/ppermute | solution.py:311

commit v9 on v8

--- a/solution.py
+++ b/solution.py
@@ -176,6 +176,23 @@
         scales[rows:, spans[a]] = (scale - scale_high.astype(F32)).astype(BF16)
 
 
+def add_rows(tiles):
+    size = len(tiles)
+    row = lax.broadcasted_iota(I32, tiles[0].shape, 0)
+    step = size // 2
+    while step >= 1:
+        tiles = [
+            jnp.where(
+                row & step == 0,
+                low + pltpu.roll(low, size - step, axis=0),
+                high + pltpu.roll(high, step, axis=0),
+            )
+            for low, high in zip(tiles[:step], tiles[step:])
+        ]
+        step //= 2
+    return tiles[0]
+
+
 def correlate_kernel(
     length, order, arrived, shifted, scales, stacked, frames, waves, traces, toeplitz, sums
 ):
@@ -249,13 +266,11 @@
                     ready = slice(done * GROUP, (done + 1) * GROUP)
                     mine = (template[ready] == t).astype(F32)
                     total = total + traces[ready, :] * jnp.concatenate([mine] * blocks, axis=1)
-                sums[t] = total
-    for k, t in enumerate(order):
-        lines = [
-            jnp.sum(sums[t, :, a * LANE : (a + 1) * LANE], axis=0, keepdims=True)
-            for a in range(blocks)
-        ]
-        stacked[k] = jnp.concatenate(lines, axis=0)
+                if g + 1 < positions // GROUP:
+                    sums[t] = total
+                else:
+                    tiles = [total[:, a * LANE : (a + 1) * LANE] for a in range(blocks)]
+                    stacked[order.index(t)] = add_rows(tiles)
 
 
 def per_device(window, prior, waves, chan_list, chan_count, station_row):

time: 27.5 us -> 27.5 us (level)
  no operation moved by 1% of the time
where the time goes in v9:
time: 27.5 us; the launch traced here: 27.3 us
  starting transfers between devices  9.71 us (35%)
  blocking collectives  8.19 us (30%)
  Pallas kernels  5.43 us (20%)
  waiting for transfers between devices  3.27 us (12%)
  other arithmetic  0.6 us (2%)
    all_to_all x1, blocking collectives, per_device(): lax.all_to_all(stacked, 'sta', split_axis=0, concat_axis=0, tiled=True, a...  8.19 us
    all_to_all x1, starting transfers between devices, per_device(): lax.all_to_all(sent.reshape(sta_size, positions // sta_size, width), 'sta...  7.99 us
    ppermute x3, waiting for transfers between devices, per_device(): pieces = pieces + [lax.ppermute(piece, 'tpl', pairs) for piece in pieces]  2.95 us
    pallas_call x1, Pallas kernels, per_device(): pl.pallas_call(functools.partial(correlate_kernel, length, templates), ou...  2.73 us
    pallas_call x1, Pallas kernels, per_device(): pl.pallas_call(functools.partial(route_kernel, sta_size, block_rows), out...  2.23 us
    ppermute x3, starting transfers between devices, per_device(): pieces = pieces + [lax.ppermute(piece, 'tpl', pairs) for piece in pieces]  1.72 us
    reduce_sum x1, other arithmetic, per_device(): return jnp.sum(parts, axis=0).reshape(each, lags)  0.6 us
  transfers between devices with their start and end apart: 4, of which 3 were waited for; matrix products, arithmetic and copies ran while one was open for 0% of the time, Pallas kernels for 2%

profile of v9, /device:TPU:0, one launch (start us, length us, event | category | flops | bytes accessed | tf_op | source)
XLA Modules:
  0.0 27.3 jit_solution(9355888425631278282)
XLA Ops:
  0.0 2.2 %route.1 = bf16[128,640]{1,0:T(8,128)(2,1)} custom-call(s32[1]{0:T(128)} %bitcast.sta_pos, bf16[128,600]{1,0:T(8,128)(2,1)} %bitcast.9, s32[8,16]{1,0:T(8,128)} %chan_list_in.1, s32[8]{0:T(128)} %chan_count_in.1, s32[1,128]{1,0:T(1,128)} %bitcast.10), custom_call_target="tpu_custom_call" | custom-call | tf_op jit(solution)/shard_map/route/pallas_call | solution.py:290
  2.2 0.0 copy-start.1
  2.2 0.0 copy-start
  2.3 8.0 %all-to-all-start = ((bf16[8,16,640]{2,1,0:T(8,128)(2,1)}), bf16[8,16,640]{2,1,0:T(8,128)(2,1)S(1)}, u32[]{:S(2)}, u32[]{:S(2)}) async-start(bf16[8,16,640]{2,1,0:T(8,128)(2,1)} %bitcast.8), calls=%async_computation | async-start | bytes 327680 | tf_op jit(solution)/shard_map/all_to_all | solution.py:312
  10.2 0.0 copy-done.1
  10.2 0.4 %collective-permute-start = (bf16[48,256]{1,0:T(8,128)(2,1)S(1)}, bf16[48,256]{1,0:T(8,128)(2,1)S(1)}, u32[]{:S(2)}, u32[]{:S(2)}) collective-permute-start(bf16[48,256]{1,0:T(8,128)(2,1)S(1)} %copy-done.1), channel_id=1, source_target_pairs={{0,3},{1,2},{2,1},{3,0},{4,7},{5,6},{6,5},{7,4},{8,11},{9,10},{10,... | collective-permute-start | bytes 73736 | tf_op jit(solution)/shard_map/ppermute | solution.py:326
  10.6 1.2 %collective-permute-start.1 = (bf16[48,256]{1,0:T(8,128)(2,1)S(1)}, bf16[48,256]{1,0:T(8,128)(2,1)S(1)}, u32[]{:S(2)}, u32[]{:S(2)}) collective-permute-start(bf16[48,256]{1,0:T(8,128)(2,1)S(1)} %copy-done.1), channel_id=1, source_target_pairs={{0,1},{1,0},{2,3},{3,2},{4,5},{5,4},{6,7},{7,6},{8,9},{9,8},{10,11... | collective-permute-start | bytes 73736 | tf_op jit(solution)/shard_map/ppermute | solution.py:326
  11.9 1.9 %collective-permute-done.refs_1_ = bf16[48,256]{1,0:T(8,128)(2,1)S(1)} collective-permute-done((bf16[48,256]{1,0:T(8,128)(2,1)S(1)}, bf16[48,256]{1,0:T(8,128)(2,1)S(1)}, u32[]{:S(2)}, u32[]{:S(2)}) %collective-permute-start) | collective-permute-done | bytes 24608 | tf_op jit(solution)/shard_map/ppermute | solution.py:326
  13.7 0.1 collective-permute-start.2
  13.8 0.0 collective-permute-done.1.refs_2_
  13.8 1.1 %collective-permute-done.2.refs_3_ = bf16[48,256]{1,0:T(8,128)(2,1)S(1)} collective-permute-done((bf16[48,256]{1,0:T(8,128)(2,1)S(1)}, bf16[48,256]{1,0:T(8,128)(2,1)S(1)}, u32[]{:S(2)}, u32[]{:S(2)}) %collective-permute-start.2) | collective-permute-done | bytes 24608 | tf_op jit(solution)/shard_map/ppermute | solution.py:326
  14.9 0.0 copy-done
  14.9 0.5 %prepare.1 = (bf16[192,1536]{1,0:T(8,128)(2,1)S(1)}, bf16[96,1024]{1,0:T(8,128)(2,1)S(1)}) custom-call(s32[1]{0:T(128)} %bitcast.5.tpl_pos, bf16[48,599]{1,0:T(8,128)(2,1)S(1)} %copy-done, bf16[48,256]{1,0:T(8,128)(2,1)S(1)} %copy-done.1, bf16[48,256]{1,0:T(8,128)(2,1)S(1)} %collective-permute-done.refs_1_, ...), custom_call_target="tpu_custom_call" | custom-call | tf_op jit(solution)/shard_map/prepare/pallas_call | solution.py:331
  15.4 0.3 %all-to-all-done = bf16[8,16,640]{2,1,0:T(8,128)(2,1)S(1)} async-done(((bf16[8,16,640]{2,1,0:T(8,128)(2,1)}), bf16[8,16,640]{2,1,0:T(8,128)(2,1)S(1)}, u32[]{:S(2)}, u32[]{:S(2)}) %all-to-all-start) | async-done | bytes 163872 | tf_op jit(solution)/shard_map/all_to_all | solution.py:312
  15.7 2.7 %correlate.1 = f32[8,8,128]{2,1,0:T(8,128)S(1)} custom-call(bf16[128,640]{1,0:T(8,128)(2,1)S(1)} %bitcast.7, bf16[192,1536]{1,0:T(8,128)(2,1)S(1)} %get-tuple-element.7.shifted, bf16[96,1024]{1,0:T(8,128)(2,1)S(1)} %get-tuple-element.8.scales), custom_call_target="tpu_custom_call" | custom-call | tf_op jit(solution)/shard_map/correlate/pallas_call | solution.py:346
  18.5 8.2 %all_to_all.10 = f32[8,8,128]{2,1,0:T(8,128)S(1)} all-to-all(f32[8,8,128]{2,1,0:T(8,128)S(1)} %correlate.1), channel_id=1, replica_groups={{16,8,0,24,20,12,4,28},{17,9,1,25,21,13,5,29},{18,10,2,26,22,14,6,30},{..., dimensions={0} | all-to-all | bytes 65536 | tf_op jit(solution)/shard_map/all_to_all | solution.py:361
  26.7 0.6 %reduce_sum.9 = f32[8,128]{1,0:T(8,128)} reduce(f32[8,8,128]{2,1,0:T(8,128)S(1)} %all_to_all.10, f32[]{:T(128)} %constant.10.clone.1), dimensions={0}, to_apply=%region_0.0 | reduce | flops 7168 | bytes 36868 | tf_op jit(solution)/shard_map/reduce_sum | solution.py:365
Async XLA Ops:
  2.2 8.0 %copy-start.1 = (bf16[48,256]{1,0:T(8,128)(2,1)S(1)}, bf16[48,256]{1,0:T(8,128)(2,1)}, u32[]{:S(2)}) copy-start(bf16[48,256]{1,0:T(8,128)(2,1)} %refs_0_.1) | copy-start | bytes 73732
  2.2 12.7 %copy-start = (bf16[48,599]{1,0:T(8,128)(2,1)S(1)}, bf16[48,599]{1,0:T(8,128)(2,1)}, u32[]{:S(2)}) copy-start(bf16[48,599]{1,0:T(8,128)(2,1)} %prior.1) | copy-start | bytes 172516
  2.3 13.5 %all-to-all-start = ((bf16[8,16,640]{2,1,0:T(8,128)(2,1)}), bf16[8,16,640]{2,1,0:T(8,128)(2,1)S(1)}, u32[]{:S(2)}, u32[]{:S(2)}) async-start(bf16[8,16,640]{2,1,0:T(8,128)(2,1)} %bitcast.8), calls=%async_computation | async-start | bytes 327680 | tf_op jit(solution)/shard_map/all_to_all | solution.py:312
  10.2 3.5 %collective-permute-start = (bf16[48,256]{1,0:T(8,128)(2,1)S(1)}, bf16[48,256]{1,0:T(8,128)(2,1)S(1)}, u32[]{:S(2)}, u32[]{:S(2)}) collective-permute-start(bf16[48,256]{1,0:T(8,128)(2,1)S(1)} %copy-done.1), channel_id=1, source_target_pairs={{0,3},{1,2},{2,1},{3,0},{4,7},{5,6},{6,5},{7,4},{8,11},{9,10},{10,... | collective-permute-start | bytes 73736 | tf_op jit(solution)/shard_map/ppermute | solution.py:326
  10.6 3.2 %collective-permute-start.1 = (bf16[48,256]{1,0:T(8,128)(2,1)S(1)}, bf16[48,256]{1,0:T(8,128)(2,1)S(1)}, u32[]{:S(2)}, u32[]{:S(2)}) collective-permute-start(bf16[48,256]{1,0:T(8,128)(2,1)S(1)} %copy-done.1), channel_id=1, source_target_pairs={{0,1},{1,0},{2,3},{3,2},{4,5},{5,4},{6,7},{7,6},{8,9},{9,8},{10,11... | collective-permute-start | bytes 73736 | tf_op jit(solution)/shard_map/ppermute | solution.py:326
  13.7 1.2 %collective-permute-start.2 = (bf16[48,256]{1,0:T(8,128)(2,1)S(1)}, bf16[48,256]{1,0:T(8,128)(2,1)S(1)}, u32[]{:S(2)}, u32[]{:S(2)}) collective-permute-start(bf16[48,256]{1,0:T(8,128)(2,1)S(1)} %collective-permute-done.refs_1_), channel_id=1, source_target_pairs={{0,1},{1,0},{2,3},{3,2},{4,5},{5,4},{6,7},{7,6},{8,9},{9,8},{10,11... | collective-permute-start | bytes 73736 | tf_op jit(solution)/shard_map/ppermute | solution.py:326

commit v10 on v9

--- a/solution.py
+++ b/solution.py
@@ -14,6 +14,7 @@
 CHUNK = 1
 TURNS = LANE // STEP
 MIB = 1 << 20
+PARTS = 4
 F32, BF16, I32 = jnp.float32, jnp.bfloat16, jnp.int32
 
 
@@ -57,6 +58,8 @@
     padded,
     arrivals,
 ):
+    quarter = waves.shape[0] // PARTS
+    parts = [pl.ds(i * quarter, quarter) for i in range(PARTS)]
     copies = [
         pltpu.make_async_copy(source, target, arrivals.at[i])
         for i, (source, target) in enumerate(
@@ -64,7 +67,7 @@
                 (chan_list_in, chan_list),
                 (station_row_in, station_row),
                 (chan_count_in, chan_count),
-                (waves_in, waves),
+                *((waves_in.at[part], waves.at[part]) for part in parts),
             )
         )
     ]
@@ -115,7 +118,8 @@
     count = jnp.zeros((positions, 1), I32)
     for t in range(group_size):
         count = jnp.where(spot // slot_count == t, chan_count[t], count)
-    copies[3].wait()
+    for copy in copies[3:]:
+        copy.wait()
     padded[:, :length] = waves[...].astype(F32)
     raw = padded[...]
     listed = (slot < count).astype(F32)
@@ -299,7 +303,7 @@
             pltpu.VMEM((1, station_row.shape[0]), I32),
             pltpu.VMEM((group_size, LANE), I32),
             pltpu.VMEM((positions, width), F32),
-            pltpu.SemaphoreType.DMA((4,)),
+            pltpu.SemaphoreType.DMA((3 + PARTS,)),
         ],
         name="route",
     )(

time: 27.5 us -> 27.6 us (level)
  no operation moved by 1% of the time
where the time goes in v10:
time: 27.6 us; the launch traced here: 27.3 us
  starting transfers between devices  9.71 us (35%)
  blocking collectives  8.19 us (30%)
  Pallas kernels  5.46 us (20%)
  waiting for transfers between devices  3.27 us (12%)
  other arithmetic  0.6 us (2%)
    all_to_all x1, blocking collectives, per_device(): lax.all_to_all(stacked, 'sta', split_axis=0, concat_axis=0, tiled=True, a...  8.19 us
    all_to_all x1, starting transfers between devices, per_device(): lax.all_to_all(sent.reshape(sta_size, positions // sta_size, width), 'sta...  7.98 us
    ppermute x3, waiting for transfers between devices, per_device(): pieces = pieces + [lax.ppermute(piece, 'tpl', pairs) for piece in pieces]  2.93 us
    pallas_call x1, Pallas kernels, per_device(): pl.pallas_call(functools.partial(correlate_kernel, length, templates), ou...  2.73 us
    pallas_call x1, Pallas kernels, per_device(): pl.pallas_call(functools.partial(route_kernel, sta_size, block_rows), out...  2.26 us
    ppermute x3, starting transfers between devices, per_device(): pieces = pieces + [lax.ppermute(piece, 'tpl', pairs) for piece in pieces]  1.73 us
    reduce_sum x1, other arithmetic, per_device(): return jnp.sum(parts, axis=0).reshape(each, lags)  0.6 us
  transfers between devices with their start and end apart: 4, of which 3 were waited for; matrix products, arithmetic and copies ran while one was open for 0% of the time, Pallas kernels for 2%

profile of v10, /device:TPU:0, one launch (start us, length us, event | category | flops | bytes accessed | tf_op | source)
XLA Modules:
  0.0 27.3 jit_solution(9752274474542900087)
XLA Ops:
  0.0 2.3 %route.1 = bf16[128,640]{1,0:T(8,128)(2,1)} custom-call(s32[1]{0:T(128)} %bitcast.sta_pos, bf16[128,600]{1,0:T(8,128)(2,1)} %bitcast.9, s32[8,16]{1,0:T(8,128)} %chan_list_in.1, s32[8]{0:T(128)} %chan_count_in.1, s32[1,128]{1,0:T(1,128)} %bitcast.10), custom_call_target="tpu_custom_call" | custom-call | tf_op jit(solution)/shard_map/route/pallas_call | solution.py:294
  2.3 0.0 copy-start.1
  2.3 0.0 copy-start
  2.3 8.0 %all-to-all-start = ((bf16[8,16,640]{2,1,0:T(8,128)(2,1)}), bf16[8,16,640]{2,1,0:T(8,128)(2,1)S(1)}, u32[]{:S(2)}, u32[]{:S(2)}) async-start(bf16[8,16,640]{2,1,0:T(8,128)(2,1)} %bitcast.8), calls=%async_computation | async-start | bytes 327680 | tf_op jit(solution)/shard_map/all_to_all | solution.py:316
  10.3 0.0 copy-done.1
  10.3 0.4 %collective-permute-start = (bf16[48,256]{1,0:T(8,128)(2,1)S(1)}, bf16[48,256]{1,0:T(8,128)(2,1)S(1)}, u32[]{:S(2)}, u32[]{:S(2)}) collective-permute-start(bf16[48,256]{1,0:T(8,128)(2,1)S(1)} %copy-done.1), channel_id=1, source_target_pairs={{0,3},{1,2},{2,1},{3,0},{4,7},{5,6},{6,5},{7,4},{8,11},{9,10},{10,... | collective-permute-start | bytes 73736 | tf_op jit(solution)/shard_map/ppermute | solution.py:330
  10.6 1.2 %collective-permute-start.1 = (bf16[48,256]{1,0:T(8,128)(2,1)S(1)}, bf16[48,256]{1,0:T(8,128)(2,1)S(1)}, u32[]{:S(2)}, u32[]{:S(2)}) collective-permute-start(bf16[48,256]{1,0:T(8,128)(2,1)S(1)} %copy-done.1), channel_id=1, source_target_pairs={{0,1},{1,0},{2,3},{3,2},{4,5},{5,4},{6,7},{7,6},{8,9},{9,8},{10,11... | collective-permute-start | bytes 73736 | tf_op jit(solution)/shard_map/ppermute | solution.py:330
  11.9 1.9 %collective-permute-done.refs_1_ = bf16[48,256]{1,0:T(8,128)(2,1)S(1)} collective-permute-done((bf16[48,256]{1,0:T(8,128)(2,1)S(1)}, bf16[48,256]{1,0:T(8,128)(2,1)S(1)}, u32[]{:S(2)}, u32[]{:S(2)}) %collective-permute-start) | collective-permute-done | bytes 24608 | tf_op jit(solution)/shard_map/ppermute | solution.py:330
  13.7 0.1 collective-permute-start.2
  13.9 0.0 collective-permute-done.1.refs_2_
  13.9 1.1 %collective-permute-done.2.refs_3_ = bf16[48,256]{1,0:T(8,128)(2,1)S(1)} collective-permute-done((bf16[48,256]{1,0:T(8,128)(2,1)S(1)}, bf16[48,256]{1,0:T(8,128)(2,1)S(1)}, u32[]{:S(2)}, u32[]{:S(2)}) %collective-permute-start.2) | collective-permute-done | bytes 24608 | tf_op jit(solution)/shard_map/ppermute | solution.py:330
  14.9 0.0 copy-done
  14.9 0.5 %prepare.1 = (bf16[192,1536]{1,0:T(8,128)(2,1)S(1)}, bf16[96,1024]{1,0:T(8,128)(2,1)S(1)}) custom-call(s32[1]{0:T(128)} %bitcast.5.tpl_pos, bf16[48,599]{1,0:T(8,128)(2,1)S(1)} %copy-done, bf16[48,256]{1,0:T(8,128)(2,1)S(1)} %copy-done.1, bf16[48,256]{1,0:T(8,128)(2,1)S(1)} %collective-permute-done.refs_1_, ...), custom_call_target="tpu_custom_call" | custom-call | tf_op jit(solution)/shard_map/prepare/pallas_call | solution.py:335
  15.4 0.3 %all-to-all-done = bf16[8,16,640]{2,1,0:T(8,128)(2,1)S(1)} async-done(((bf16[8,16,640]{2,1,0:T(8,128)(2,1)}), bf16[8,16,640]{2,1,0:T(8,128)(2,1)S(1)}, u32[]{:S(2)}, u32[]{:S(2)}) %all-to-all-start) | async-done | bytes 163872 | tf_op jit(solution)/shard_map/all_to_all | solution.py:316
  15.8 2.7 %correlate.1 = f32[8,8,128]{2,1,0:T(8,128)S(1)} custom-call(bf16[128,640]{1,0:T(8,128)(2,1)S(1)} %bitcast.7, bf16[192,1536]{1,0:T(8,128)(2,1)S(1)} %get-tuple-element.7.shifted, bf16[96,1024]{1,0:T(8,128)(2,1)S(1)} %get-tuple-element.8.scales), custom_call_target="tpu_custom_call" | custom-call | tf_op jit(solution)/shard_map/correlate/pallas_call | solution.py:350
  18.5 8.2 %all_to_all.10 = f32[8,8,128]{2,1,0:T(8,128)S(1)} all-to-all(f32[8,8,128]{2,1,0:T(8,128)S(1)} %correlate.1), channel_id=1, replica_groups={{16,8,0,24,20,12,4,28},{17,9,1,25,21,13,5,29},{18,10,2,26,22,14,6,30},{..., dimensions={0} | all-to-all | bytes 65536 | tf_op jit(solution)/shard_map/all_to_all | solution.py:365
  26.7 0.6 %reduce_sum.9 = f32[8,128]{1,0:T(8,128)} reduce(f32[8,8,128]{2,1,0:T(8,128)S(1)} %all_to_all.10, f32[]{:T(128)} %constant.10.clone.1), dimensions={0}, to_apply=%region_0.0 | reduce | flops 7168 | bytes 36868 | tf_op jit(solution)/shard_map/reduce_sum | solution.py:369
Async XLA Ops:
  2.3 8.0 %copy-start.1 = (bf16[48,256]{1,0:T(8,128)(2,1)S(1)}, bf16[48,256]{1,0:T(8,128)(2,1)}, u32[]{:S(2)}) copy-start(bf16[48,256]{1,0:T(8,128)(2,1)} %refs_0_.1) | copy-start | bytes 73732
  2.3 12.7 %copy-start = (bf16[48,599]{1,0:T(8,128)(2,1)S(1)}, bf16[48,599]{1,0:T(8,128)(2,1)}, u32[]{:S(2)}) copy-start(bf16[48,599]{1,0:T(8,128)(2,1)} %prior.1) | copy-start | bytes 172516
  2.3 13.5 %all-to-all-start = ((bf16[8,16,640]{2,1,0:T(8,128)(2,1)}), bf16[8,16,640]{2,1,0:T(8,128)(2,1)S(1)}, u32[]{:S(2)}, u32[]{:S(2)}) async-start(bf16[8,16,640]{2,1,0:T(8,128)(2,1)} %bitcast.8), calls=%async_computation | async-start | bytes 327680 | tf_op jit(solution)/shard_map/all_to_all | solution.py:316
  10.3 3.5 %collective-permute-start = (bf16[48,256]{1,0:T(8,128)(2,1)S(1)}, bf16[48,256]{1,0:T(8,128)(2,1)S(1)}, u32[]{:S(2)}, u32[]{:S(2)}) collective-permute-start(bf16[48,256]{1,0:T(8,128)(2,1)S(1)} %copy-done.1), channel_id=1, source_target_pairs={{0,3},{1,2},{2,1},{3,0},{4,7},{5,6},{6,5},{7,4},{8,11},{9,10},{10,... | collective-permute-start | bytes 73736 | tf_op jit(solution)/shard_map/ppermute | solution.py:330
  10.6 3.2 %collective-permute-start.1 = (bf16[48,256]{1,0:T(8,128)(2,1)S(1)}, bf16[48,256]{1,0:T(8,128)(2,1)S(1)}, u32[]{:S(2)}, u32[]{:S(2)}) collective-permute-start(bf16[48,256]{1,0:T(8,128)(2,1)S(1)} %copy-done.1), channel_id=1, source_target_pairs={{0,1},{1,0},{2,3},{3,2},{4,5},{5,4},{6,7},{7,6},{8,9},{9,8},{10,11... | collective-permute-start | bytes 73736 | tf_op jit(solution)/shard_map/ppermute | solution.py:330
  13.7 1.2 %collective-permute-start.2 = (bf16[48,256]{1,0:T(8,128)(2,1)S(1)}, bf16[48,256]{1,0:T(8,128)(2,1)S(1)}, u32[]{:S(2)}, u32[]{:S(2)}) collective-permute-start(bf16[48,256]{1,0:T(8,128)(2,1)S(1)} %collective-permute-done.refs_1_), channel_id=1, source_target_pairs={{0,1},{1,0},{2,3},{3,2},{4,5},{5,4},{6,7},{7,6},{8,9},{9,8},{10,11... | collective-permute-start | bytes 73736 | tf_op jit(solution)/shard_map/ppermute | solution.py:330

commit v11 on v9

--- a/solution.py
+++ b/solution.py
@@ -27,7 +27,7 @@
 
 def waves_order(size):
     if size == 8:
-        return [3, 0, 1, 4, 5, 7, 2, 6]
+        return [3, 0, 1, 5, 4, 7, 2, 6]
     return [(i + size // 2 - 1) % size for i in range(size)]
 
 

time: 27.5 us -> 27.5 us (level)
  no operation moved by 1% of the time
where the time goes in v11:
time: 27.5 us; the launch traced here: 27.3 us
  starting transfers between devices  9.71 us (35%)
  blocking collectives  8.19 us (30%)
  Pallas kernels  5.43 us (20%)
  waiting for transfers between devices  3.27 us (12%)
  other arithmetic  0.6 us (2%)
    all_to_all x1, blocking collectives, per_device(): lax.all_to_all(stacked, 'sta', split_axis=0, concat_axis=0, tiled=True, a...  8.19 us
    all_to_all x1, starting transfers between devices, per_device(): lax.all_to_all(sent.reshape(sta_size, positions // sta_size, width), 'sta...  7.99 us
    ppermute x3, waiting for transfers between devices, per_device(): pieces = pieces + [lax.ppermute(piece, 'tpl', pairs) for piece in pieces]  2.95 us
    pallas_call x1, Pallas kernels, per_device(): pl.pallas_call(functools.partial(correlate_kernel, length, templates), ou...  2.73 us
    pallas_call x1, Pallas kernels, per_device(): pl.pallas_call(functools.partial(route_kernel, sta_size, block_rows), out...  2.23 us
    ppermute x3, starting transfers between devices, per_device(): pieces = pieces + [lax.ppermute(piece, 'tpl', pairs) for piece in pieces]  1.72 us
    reduce_sum x1, other arithmetic, per_device(): return jnp.sum(parts, axis=0).reshape(each, lags)  0.6 us
  transfers between devices with their start and end apart: 4, of which 3 were waited for; matrix products, arithmetic and copies ran while one was open for 0% of the time, Pallas kernels for 2%

profile of v11, /device:TPU:0, one launch (start us, length us, event | category | flops | bytes accessed | tf_op | source)
XLA Modules:
  0.0 27.3 jit_solution(14368030487070884026)
XLA Ops:
  0.0 2.2 %route.1 = bf16[128,640]{1,0:T(8,128)(2,1)} custom-call(s32[1]{0:T(128)} %bitcast.sta_pos, bf16[128,600]{1,0:T(8,128)(2,1)} %bitcast.9, s32[8,16]{1,0:T(8,128)} %chan_list_in.1, s32[8]{0:T(128)} %chan_count_in.1, s32[1,128]{1,0:T(1,128)} %bitcast.10), custom_call_target="tpu_custom_call" | custom-call | tf_op jit(solution)/shard_map/route/pallas_call | solution.py:290
  2.2 0.0 copy-start.1
  2.2 0.0 copy-start
  2.3 8.0 %all-to-all-start = ((bf16[8,16,640]{2,1,0:T(8,128)(2,1)}), bf16[8,16,640]{2,1,0:T(8,128)(2,1)S(1)}, u32[]{:S(2)}, u32[]{:S(2)}) async-start(bf16[8,16,640]{2,1,0:T(8,128)(2,1)} %bitcast.8), calls=%async_computation | async-start | bytes 327680 | tf_op jit(solution)/shard_map/all_to_all | solution.py:312
  10.2 0.0 copy-done.1
  10.2 0.4 %collective-permute-start = (bf16[48,256]{1,0:T(8,128)(2,1)S(1)}, bf16[48,256]{1,0:T(8,128)(2,1)S(1)}, u32[]{:S(2)}, u32[]{:S(2)}) collective-permute-start(bf16[48,256]{1,0:T(8,128)(2,1)S(1)} %copy-done.1), channel_id=1, source_target_pairs={{0,3},{1,2},{2,1},{3,0},{4,7},{5,6},{6,5},{7,4},{8,11},{9,10},{10,... | collective-permute-start | bytes 73736 | tf_op jit(solution)/shard_map/ppermute | solution.py:326
  10.6 1.2 %collective-permute-start.1 = (bf16[48,256]{1,0:T(8,128)(2,1)S(1)}, bf16[48,256]{1,0:T(8,128)(2,1)S(1)}, u32[]{:S(2)}, u32[]{:S(2)}) collective-permute-start(bf16[48,256]{1,0:T(8,128)(2,1)S(1)} %copy-done.1), channel_id=1, source_target_pairs={{0,1},{1,0},{2,3},{3,2},{4,5},{5,4},{6,7},{7,6},{8,9},{9,8},{10,11... | collective-permute-start | bytes 73736 | tf_op jit(solution)/shard_map/ppermute | solution.py:326
  11.9 1.9 %collective-permute-done.refs_1_ = bf16[48,256]{1,0:T(8,128)(2,1)S(1)} collective-permute-done((bf16[48,256]{1,0:T(8,128)(2,1)S(1)}, bf16[48,256]{1,0:T(8,128)(2,1)S(1)}, u32[]{:S(2)}, u32[]{:S(2)}) %collective-permute-start) | collective-permute-done | bytes 24608 | tf_op jit(solution)/shard_map/ppermute | solution.py:326
  13.7 0.1 collective-permute-start.2
  13.8 0.0 collective-permute-done.1.refs_2_
  13.8 1.1 %collective-permute-done.2.refs_3_ = bf16[48,256]{1,0:T(8,128)(2,1)S(1)} collective-permute-done((bf16[48,256]{1,0:T(8,128)(2,1)S(1)}, bf16[48,256]{1,0:T(8,128)(2,1)S(1)}, u32[]{:S(2)}, u32[]{:S(2)}) %collective-permute-start.2) | collective-permute-done | bytes 24608 | tf_op jit(solution)/shard_map/ppermute | solution.py:326
  14.9 0.0 copy-done
  14.9 0.5 %prepare.1 = (bf16[192,1536]{1,0:T(8,128)(2,1)S(1)}, bf16[96,1024]{1,0:T(8,128)(2,1)S(1)}) custom-call(s32[1]{0:T(128)} %bitcast.5.tpl_pos, bf16[48,599]{1,0:T(8,128)(2,1)S(1)} %copy-done, bf16[48,256]{1,0:T(8,128)(2,1)S(1)} %copy-done.1, bf16[48,256]{1,0:T(8,128)(2,1)S(1)} %collective-permute-done.refs_1_, ...), custom_call_target="tpu_custom_call" | custom-call | tf_op jit(solution)/shard_map/prepare/pallas_call | solution.py:331
  15.4 0.3 %all-to-all-done = bf16[8,16,640]{2,1,0:T(8,128)(2,1)S(1)} async-done(((bf16[8,16,640]{2,1,0:T(8,128)(2,1)}), bf16[8,16,640]{2,1,0:T(8,128)(2,1)S(1)}, u32[]{:S(2)}, u32[]{:S(2)}) %all-to-all-start) | async-done | bytes 163872 | tf_op jit(solution)/shard_map/all_to_all | solution.py:312
  15.7 2.7 %correlate.1 = f32[8,8,128]{2,1,0:T(8,128)S(1)} custom-call(bf16[128,640]{1,0:T(8,128)(2,1)S(1)} %bitcast.7, bf16[192,1536]{1,0:T(8,128)(2,1)S(1)} %get-tuple-element.7.shifted, bf16[96,1024]{1,0:T(8,128)(2,1)S(1)} %get-tuple-element.8.scales), custom_call_target="tpu_custom_call" | custom-call | tf_op jit(solution)/shard_map/correlate/pallas_call | solution.py:346
  18.5 8.2 %all_to_all.10 = f32[8,8,128]{2,1,0:T(8,128)S(1)} all-to-all(f32[8,8,128]{2,1,0:T(8,128)S(1)} %correlate.1), channel_id=1, replica_groups={{16,8,0,24,20,12,4,28},{17,9,1,25,21,13,5,29},{18,10,2,26,22,14,6,30},{..., dimensions={0} | all-to-all | bytes 65536 | tf_op jit(solution)/shard_map/all_to_all | solution.py:361
  26.7 0.6 %reduce_sum.9 = f32[8,128]{1,0:T(8,128)} reduce(f32[8,8,128]{2,1,0:T(8,128)S(1)} %all_to_all.10, f32[]{:T(128)} %constant.10.clone.1), dimensions={0}, to_apply=%region_0.0 | reduce | flops 7168 | bytes 36868 | tf_op jit(solution)/shard_map/reduce_sum | solution.py:365
Async XLA Ops:
  2.2 8.0 %copy-start.1 = (bf16[48,256]{1,0:T(8,128)(2,1)S(1)}, bf16[48,256]{1,0:T(8,128)(2,1)}, u32[]{:S(2)}) copy-start(bf16[48,256]{1,0:T(8,128)(2,1)} %refs_0_.1) | copy-start | bytes 73732
  2.2 12.7 %copy-start = (bf16[48,599]{1,0:T(8,128)(2,1)S(1)}, bf16[48,599]{1,0:T(8,128)(2,1)}, u32[]{:S(2)}) copy-start(bf16[48,599]{1,0:T(8,128)(2,1)} %prior.1) | copy-start | bytes 172516
  2.3 13.5 %all-to-all-start = ((bf16[8,16,640]{2,1,0:T(8,128)(2,1)}), bf16[8,16,640]{2,1,0:T(8,128)(2,1)S(1)}, u32[]{:S(2)}, u32[]{:S(2)}) async-start(bf16[8,16,640]{2,1,0:T(8,128)(2,1)} %bitcast.8), calls=%async_computation | async-start | bytes 327680 | tf_op jit(solution)/shard_map/all_to_all | solution.py:312
  10.2 3.5 %collective-permute-start = (bf16[48,256]{1,0:T(8,128)(2,1)S(1)}, bf16[48,256]{1,0:T(8,128)(2,1)S(1)}, u32[]{:S(2)}, u32[]{:S(2)}) collective-permute-start(bf16[48,256]{1,0:T(8,128)(2,1)S(1)} %copy-done.1), channel_id=1, source_target_pairs={{0,3},{1,2},{2,1},{3,0},{4,7},{5,6},{6,5},{7,4},{8,11},{9,10},{10,... | collective-permute-start | bytes 73736 | tf_op jit(solution)/shard_map/ppermute | solution.py:326
  10.6 3.2 %collective-permute-start.1 = (bf16[48,256]{1,0:T(8,128)(2,1)S(1)}, bf16[48,256]{1,0:T(8,128)(2,1)S(1)}, u32[]{:S(2)}, u32[]{:S(2)}) collective-permute-start(bf16[48,256]{1,0:T(8,128)(2,1)S(1)} %copy-done.1), channel_id=1, source_target_pairs={{0,1},{1,0},{2,3},{3,2},{4,5},{5,4},{6,7},{7,6},{8,9},{9,8},{10,11... | collective-permute-start | bytes 73736 | tf_op jit(solution)/shard_map/ppermute | solution.py:326
  13.7 1.2 %collective-permute-start.2 = (bf16[48,256]{1,0:T(8,128)(2,1)S(1)}, bf16[48,256]{1,0:T(8,128)(2,1)S(1)}, u32[]{:S(2)}, u32[]{:S(2)}) collective-permute-start(bf16[48,256]{1,0:T(8,128)(2,1)S(1)} %collective-permute-done.refs_1_), channel_id=1, source_target_pairs={{0,1},{1,0},{2,3},{3,2},{4,5},{5,4},{6,7},{7,6},{8,9},{9,8},{10,11... | collective-permute-start | bytes 73736 | tf_op jit(solution)/shard_map/ppermute | solution.py:326
